TPU v7x, 32 devices: a whole 2x2x4 slice. The times are simulated.
32 devices in a mesh: groups: 2 (over y), seq: 4 (over z), beam: 4 (over x, core).
Axes of the slice: x: 2, y: 2, z: 4, core: 2. Of those that a mesh axis runs over, the one named last changes fastest.
Arguments:
- prompt_values: bfloat16 [2048, 8192], P(('groups', 'seq'), 'beam'), parts along dimension 0, may hold values from -6 to 6
- prompt_keys: bfloat16 [2048, 128], P(('groups', 'seq')), parts along dimension 0, may hold values from -0.31445312 to 0.31445312
- prompt_queries: bfloat16 [2048, 128], P(('groups', 'seq')), parts along dimension 0, may hold values from -0.31445312 to 0.31445312
- logarithm_state_decay: float32 [2048, 128], P(('groups', 'seq'), 'beam'), parts along dimension 0, may hold values from -1 to 0
- step_values: bfloat16 [8, 4, 8192], P('groups', 'beam', 'seq'), parts along dimension 0, may hold values from -6 to 6
- step_keys: bfloat16 [8, 4, 128], P('groups', 'beam'), parts along dimension 0, may hold values from -6 to 6
- step_queries: bfloat16 [8, 4, 128], P('groups', 'beam'), parts along dimension 0, may hold values from -0.31445312 to 0.31445312
- step_decay: float32 [8, 4, 128], P('groups', 'beam', 'seq'), parts along dimension 0, may hold values from -0.6 to -0.02
- step_logprob: float32 [8, 4], P('groups', 'beam'), parts along dimension 0, may hold values from -6 to -0.05
- parents: int32 [8, 4], P('groups', 'beam'), parts along dimension 0, may hold values from 0 to 3
- finished: int32 [8, 4], P('groups', 'beam'), parts along dimension 0, may hold values 0 or 1
- lengths: int32 [8], P(('groups', 'beam')), parts along dimension 0, may hold values from 1 to 59
- init_score: float32 [8], P(('groups', 'beam')), parts along dimension 0, may hold values from -20 to -2
Outputs:
- prompt_output: bfloat16 [2048, 8192], P(('groups', 'seq'), 'beam'), parts along dimension 0
- step_output: bfloat16 [8, 4, 8192], P('groups', 'beam', 'seq'), parts along dimension 0
- ranked: float32 [8, 4], P('groups', 'beam'), parts along dimension 0
- beam_states: float32 [8, 8192, 128], P(('groups', 'beam'), 'seq'), parts along dimension 0
There are 2 independent parts, one for each index of `groups`. A program takes and returns all parts, laid end to end along the dimension named above; each array names one. Nothing has to cross between parts.
All inputs are finite; a program needn't handle non-finite values. No bound on the sum of `finished` on one device may be relied on, other than what follows from the above.
Results may differ from a plain program's by a relative error of at most 0.0056.
Values sent between devices are 32-bit elements; how exact they have to be, the bound alone decides.
A program may use at most 64 MiB of HBM per device.

v0:
```python
import jax
import jax.numpy as jnp
from jax import lax
from jax.sharding import PartitionSpec as P

P_SIZE = 64
N = 128
STEPS = 4
SPAN = 256


def on_device(
    prompt_values,
    prompt_keys,
    prompt_queries,
    logarithm_state_decay,
    step_values,
    step_keys,
    step_queries,
    step_decay,
    step_logprob,
    parents,
    finished,
    lengths,
    init_score,
):
    token_rows = prompt_values.shape[0]
    head_count = logarithm_state_decay.shape[1]
    block_count = token_rows // SPAN
    values_blocks = prompt_values.reshape(block_count, SPAN, head_count, P_SIZE)
    keys_blocks = prompt_keys.reshape(block_count, SPAN, N)
    query_blocks = prompt_queries.reshape(block_count, SPAN, N)
    decay_sums = jnp.cumsum(logarithm_state_decay.reshape(block_count, SPAN, head_count), axis=1)
    lower = jnp.tril(jnp.ones((SPAN, SPAN), dtype=bool))

    def within(item):
        values_one, keys_one, query_one, sums_one = item
        scores = jnp.dot(query_one, keys_one.T, preferred_element_type=jnp.float32)
        spread = jnp.where(lower[:, :, None], sums_one[:, None, :] - sums_one[None, :, :], -jnp.inf)
        weights = (scores[:, :, None] * jnp.exp(spread)).astype(jnp.bfloat16)
        return jnp.einsum("ijh,jhp->ihp", weights, values_one, preferred_element_type=jnp.float32)

    inner_out = lax.map(within, (values_blocks, keys_blocks, query_blocks, decay_sums))
    tail_decay = jnp.exp(decay_sums[:, -1:, :] - decay_sums)
    scaled = (values_blocks * tail_decay[:, :, :, None]).astype(jnp.bfloat16)
    block_states = jnp.einsum(
        "kjhp,kjn->khpn", scaled, keys_blocks, preferred_element_type=jnp.float32
    )
    block_decay = jnp.exp(decay_sums[:, -1, :])

    def advance(carry, item):
        state_now, current_shrink_factor = carry
        single_token_decay, state_one = item
        return (
            (
                single_token_decay[:, None, None] * state_now + state_one,
                current_shrink_factor * single_token_decay,
            ),
            (state_now, current_shrink_factor),
        )

    zero_state = jnp.zeros((head_count, P_SIZE, N), jnp.float32)
    unit_decay = jnp.ones((head_count,), jnp.float32)
    (segment_finish, total_decay), (before, prior) = lax.scan(
        advance, (zero_state, unit_decay), (block_decay, block_states)
    )
    seq_index = lax.axis_index("seq")
    all_decays, all_states = (
        lax.all_gather(total_decay[None], "seq", axis=0, tiled=True),
        lax.all_gather(segment_finish[None], "seq", axis=0, tiled=True),
    )
    piece_ids = jnp.arange(all_decays.shape[0], dtype=jnp.int32)

    def collect(carry, item):
        running, mine = carry
        decay_one, state_one, piece_id = item
        mine = jnp.where(piece_id == seq_index, running, mine)
        running = decay_one[:, None, None] * running + state_one
        return ((running, mine), None)

    (full_block, arriving_input), unused = lax.scan(
        collect, (zero_state, zero_state), (all_decays, all_states, piece_ids)
    )
    starts = prior[:, :, None, None] * arriving_input[None] + before
    carried = (
        jnp.einsum(
            "kin,khpn->kihp",
            query_blocks,
            starts.astype(jnp.bfloat16),
            preferred_element_type=jnp.float32,
        )
        * jnp.exp(decay_sums)[:, :, :, None]
    )
    prompt_output = (
        (inner_out + carried).astype(jnp.bfloat16).reshape(token_rows, head_count * P_SIZE)
    )
    group_heads = step_values.shape[2] // P_SIZE
    first_head = seq_index * group_heads
    every_head = lax.all_gather(full_block, "beam", axis=0, tiled=True)
    own_heads = lax.dynamic_slice_in_dim(every_head, first_head, group_heads, 0)
    state_now = own_heads
    score_now = init_score
    length_now = lengths.astype(jnp.float32)
    step_list = []
    ranked_list = []
    for step_index in range(STEPS):
        parent_now = parents[step_index, 0]
        pieces = (
            lax.all_gather(state_now[None], "beam", axis=0, tiled=True),
            lax.all_gather(score_now, "beam", axis=0, tiled=True),
            lax.all_gather(length_now, "beam", axis=0, tiled=True),
        )
        slot_ids = jnp.arange(pieces[0].shape[0], dtype=jnp.int32)
        picked = (slot_ids == parent_now).astype(jnp.float32)
        state_part = jnp.sum(picked[:, None, None, None] * pieces[0], axis=0, keepdims=True)
        score_part = jnp.sum(picked * pieces[1]).reshape(1)
        length_part = jnp.sum(picked * pieces[2]).reshape(1)
        done = finished[step_index, 0] == 1
        live = (1 - finished[step_index]).astype(jnp.float32)
        values_now = step_values[step_index, 0].astype(jnp.float32).reshape(group_heads, P_SIZE)
        keys_now = step_keys[step_index, 0].astype(jnp.float32)
        updated = (
            jnp.exp(step_decay[step_index, 0])[:, None, None] * state_part[0]
            + values_now[:, :, None] * keys_now[None, None, :]
        )
        state_now = jnp.where(done, state_part[0], updated)
        output_now = jnp.einsum(
            "hpn,n->hp",
            state_now.astype(jnp.bfloat16),
            step_queries[step_index, 0],
            preferred_element_type=jnp.float32,
        )
        output_now = jnp.where(done, jnp.float32(0.0), output_now)
        step_list.append(output_now.reshape(1, group_heads * P_SIZE).astype(jnp.bfloat16))
        score_now = score_part + live * step_logprob[step_index]
        length_now = length_part + live
        normed = score_now / ((5.0 + length_now) / 6.0) ** 0.6
        best = lax.pmax(normed, "beam")
        ranked_list.append(normed - best)
    step_output = jnp.stack(step_list)
    ranked = jnp.stack(ranked_list)
    beam_states = state_now.reshape(1, group_heads * P_SIZE, N)
    return (prompt_output, step_output, ranked, beam_states)


def solution(mesh):
    return jax.shard_map(
        on_device,
        mesh=mesh,
        in_specs=(
            P(("groups", "seq"), "beam"),
            P(("groups", "seq"), None),
            P(("groups", "seq"), None),
            P(("groups", "seq"), "beam"),
            P("groups", "beam", "seq"),
            P("groups", "beam", None),
            P("groups", "beam", None),
            P("groups", "beam", "seq"),
            P("groups", "beam"),
            P("groups", "beam"),
            P("groups", "beam"),
            P(("groups", "beam")),
            P(("groups", "beam")),
        ),
        out_specs=(
            P(("groups", "seq"), "beam"),
            P("groups", "beam", "seq"),
            P("groups", "beam"),
            P(("groups", "beam"), "seq", None),
        ),
        check_vma=False,
    )
```

profile of v0, /device:TPU:3, one launch (start us, length us, event | category | flops | bytes accessed | tf_op | source)
XLA Modules:
  0.0 357.9 jit_solution(6325629616704435772)
XLA Ops:
  9.1 1.5 copy.50
  12.3 9.1 %all-gather = f32[4,1,32]{2,1,0:T(1,128)S(1)} all-gather(f32[1,1,32]{2,1,0:T(1,128)S(1)} %get-tuple-element.163), channel_id=2, replica_groups=mesh['groups'=2,'seq'=4,'beam'=4] {'seq'}, dimensions={0}, use_global_device_ids=true | all-gather | bytes 640 | tf_op jit(solution)/shard_map/all_gather | solution.py:69
  21.4 73.0 %all-gather.18.cloned.1.call-done = f32[128,64,128]{2,1,0:T(8,128)} async-done(((f32[32,64,128]{2,1,0:T(8,128)}), f32[128,64,128]{2,1,0:T(8,128)}) %all-gather.18.cloned.1.call-update) | async-done | bytes 4194320 | tf_op jit(solution)/shard_map/all_gather | solution.py:70
  94.4 11.8 %while.3 = (s32[]{:T(128)}, f32[32,64,128]{2,1,0:T(8,128)S(1)}, bf16[32,64,128]{2,1,0:T(8,128)(2,1)S(1)}, f32[4,32]{1,0:T(4,128)S(1)}, f32[4,32,64,128]{3,2,1,0:...) while((s32[]{:T(128)}, f32[32,64,128]{2,1,0:T(8,128)S(1)}, ...), condition=%wide.region_3.4_spmd.clone, body=%wide.region_2.3_spmd.clone.sunk | while | flops 1572868 | bytes 5243406 | solution.py:81
  95.9 1.4 bitcast_add_fusion.7
  98.9 1.4 bitcast_add_fusion.7
  101.8 1.4 bitcast_add_fusion.7
  104.8 1.4 bitcast_add_fusion.7
  107.3 32.4 %all-gather.10.cloned.1.call-done = f32[128,64,128]{2,1,0:T(8,128)} async-done(((f32[32,64,128]{2,1,0:T(8,128)}), f32[128,64,128]{2,1,0:T(8,128)}) %all-gather.10.cloned.1.call-update) | async-done | bytes 4194320 | tf_op jit(solution)/shard_map/all_gather | solution.py:99
  139.6 2.3 constant_dynamic-slice_fusion
  144.8 31.8 %all-gather.20.cloned.1.call-done = f32[128,64,128]{2,1,0:T(8,128)} async-done(((f32[32,64,128]{2,1,0:T(8,128)}), f32[128,64,128]{2,1,0:T(8,128)}) %all-gather.20.cloned.1.call-update) | async-done | bytes 4194320 | tf_op jit(solution)/shard_map/all_gather | solution.py:109
  176.6 2.9 multiply_reduce_fusion.3
  182.2 33.2 %all-gather.12.cloned.1.call-done = f32[4,32,64,128]{3,2,1,0:T(8,128)} async-done(((f32[1,32,64,128]{3,2,1,0:T(8,128)}), f32[4,32,64,128]{3,2,1,0:T(8,128)}) %all-gather.12.cloned.1.call-update) | async-done | bytes 4194320 | tf_op jit(solution)/shard_map/all_gather | solution.py:109
  215.5 2.9 multiply_reduce_fusion.2
  222.2 33.2 %all-gather.14.cloned.1.call-done = f32[4,32,64,128]{3,2,1,0:T(8,128)} async-done(((f32[1,32,64,128]{3,2,1,0:T(8,128)}), f32[4,32,64,128]{3,2,1,0:T(8,128)}) %all-gather.14.cloned.1.call-update) | async-done | bytes 4194320 | tf_op jit(solution)/shard_map/all_gather | solution.py:109
  255.4 2.9 multiply_reduce_fusion.1
  264.1 5.3 %all-reduce.11 = (f32[4]{0:T(128)S(1)}, f32[4]{0:T(128)S(1)}) all-reduce(f32[4]{0:T(128)S(1)} %dynamic-update-slice, f32[4]{0:T(128)S(1)} %convert_dynamic-update-slice_fusion), channel_id=1, replica_groups=mesh['groups'=2,'seq'=4,'beam'=4] {'beam'}, use_global_device_ids=true, to_apply=%add | all-reduce | flops 8 | bytes 64
  273.9 1.7 fusion.50
  275.6 1.4 dynamic-update-slice.2
  277.1 1.4 dynamic-update-slice.3
  278.5 7.2 %all-reduce.10 = (f32[4]{0:T(128)S(1)}, f32[4]{0:T(128)S(1)}) all-reduce(f32[4]{0:T(128)S(1)} %dynamic-update-slice.2, f32[4]{0:T(128)S(1)} %dynamic-update-slice.3), channel_id=1, replica_groups=mesh['groups'=2,'seq'=4,'beam'=4] {'beam'}, use_global_device_ids=true, to_apply=%add.2 | all-reduce | flops 8 | bytes 64
  290.7 1.7 fusion.48
  293.8 1.4 dynamic-update-slice.5
  295.2 6.1 %all-reduce.9 = (f32[4]{0:T(128)S(1)}, f32[4]{0:T(128)S(1)}) all-reduce(f32[4]{0:T(128)S(1)} %dynamic-update-slice.4, f32[4]{0:T(128)S(1)} %dynamic-update-slice.5), channel_id=1, replica_groups=mesh['groups'=2,'seq'=4,'beam'=4] {'beam'}, use_global_device_ids=true, to_apply=%add.4 | all-reduce | flops 8 | bytes 64
  306.3 1.9 fusion.46
  310.9 5.7 %all-reduce.8 = (f32[4]{0:T(128)S(1)}, f32[4]{0:T(128)S(1)}) all-reduce(f32[4]{0:T(128)S(1)} %dynamic-update-slice.6, f32[4]{0:T(128)S(1)} %dynamic-update-slice.7), channel_id=1, replica_groups=mesh['groups'=2,'seq'=4,'beam'=4] {'beam'}, use_global_device_ids=true, to_apply=%add.6 | all-reduce | flops 8 | bytes 64
  321.9 6.6 %all-reduce.12 = (f32[1]{0:T(128)}, f32[1]{0:T(128)}, f32[1]{0:T(128)}, f32[1]{0:T(128)}) all-reduce(f32[1]{0:T(128)S(6)} %div.31, f32[1]{0:T(128)} %get-tuple-element.186, f32[1]{0:T(128)} %get-tuple-element.190, f32[1]{0:T(128)} %get-tuple-element.194), channel_id=1, replica_groups=mesh['groups'=2,'seq'=4,'beam'=4] {'beam'}, use_global_device_ids=true, to_apply=%region_19.20 | all-reduce | flops 4 | bytes 32 | tf_op jit(solution)/shard_map/pmax | solution.py:138
  335.9 3.7 %fusion.7 = bf16[256,32,64]{0,2,1:T(8,128)(2,1)} fusion(f32[32,64,256]{2,1,0:T(8,128)S(1)} %fusion.13, bf16[256,32,64]{0,2,1:T(8,128)(2,1)S(1)} %bitcast.193, f32[256,32]{0,1:T(8,128)S(1)} %copy.48, f32[256,256]{1,0:T(8,128)S(1)} %fusion.51, pred[256,256]{1,0:T(8,128)(4,1)S(1)} %iota_compare_fusion, f32[256,32]{0,1:T(8,128)S(1)} %copy.53), kind=kOutput, calls=%fused_computation.16 | convolution fusion | flops 278396928 | bytes 4587520 | tf_op jit(solution)/shard_map/while/body/eval_jaxpr/ijh,jhp->ihp/dot_general | solution.py:41
  339.6 2.4 copy.54
  342.7 1.8 fusion.16
  345.3 2.9 multiply_reduce_fusion
  348.9 1.6 bitcast_select_fusion
  (132 shorter events, 42.1 us)
Async XLA Ops:
  7.2 328.1 %copy-start = (bf16[256,128]{1,0:T(8,128)(2,1)S(1)}, bf16[256,128]{1,0:T(8,128)(2,1)}, u32[]{:S(2)}) copy-start(bf16[256,128]{1,0:T(8,128)(2,1)} %param.17) | copy-start | bytes 196612
  7.2 3.6 %copy-start.5 = (bf16[256,128]{1,0:T(8,128)(2,1)S(1)}, bf16[256,128]{1,0:T(8,128)(2,1)}, u32[]{:S(2)}) copy-start(bf16[256,128]{1,0:T(8,128)(2,1)} %param.16) | copy-start | bytes 196612
  7.2 87.2 %all-gather.18.cloned.1.call-start = ((), (), s32[]{:S(2)}) async-start(), calls=%async_computation.4 | async-start | bytes 5242880 | tf_op jit(solution)/shard_map/all_gather | solution.py:70
  12.3 127.4 %all-gather.10.cloned.1.call-start = ((), (), s32[]{:S(2)}) async-start(), calls=%async_computation | async-start | bytes 5242880 | tf_op jit(solution)/shard_map/all_gather | solution.py:99
  106.2 1.0 copy-start.1
  106.2 35.8 %copy-start.6 = (bf16[4,1,2048]{2,0,1:T(4,128)(2,1)S(1)}, bf16[4,1,2048]{2,0,1:T(4,128)(2,1)}, u32[]{:S(2)}) copy-start(bf16[4,1,2048]{2,0,1:T(4,128)(2,1)} %param.19) | copy-start | bytes 49156
  106.2 35.9 %copy-start.7 = (s32[4,1]{0,1:T(1,128)S(1)}, s32[4,1]{0,1:T(1,128)}, u32[]{:S(2)}) copy-start(s32[4,1]{0,1:T(1,128)} %param.25) | copy-start | bytes 52
  106.2 37.2 %copy-start.8 = (s32[4,1]{0,1:T(1,128)S(1)}, s32[4,1]{0,1:T(1,128)}, u32[]{:S(2)}) copy-start(s32[4,1]{0,1:T(1,128)} %param.24) | copy-start | bytes 52
  106.3 38.5 %copy-start.11 = (f32[4,1,32]{2,1,0:T(1,128)S(1)}, f32[4,1,32]{2,1,0:T(1,128)}, u32[]{:S(2)}) copy-start(f32[4,1,32]{2,1,0:T(1,128)} %param.22) | copy-start | bytes 1540
  106.3 38.5 %copy-start.10 = (bf16[4,1,128]{2,0,1:T(4,128)(2,1)S(1)}, bf16[4,1,128]{2,0,1:T(4,128)(2,1)}, u32[]{:S(2)}) copy-start(bf16[4,1,128]{2,0,1:T(4,128)(2,1)} %param.20) | copy-start | bytes 3076
  107.2 69.4 %all-gather.20.cloned.1.call-start = ((), (), s32[]{:S(2)}) async-start(), calls=%async_computation.5 | async-start | bytes 5242880 | tf_op jit(solution)/shard_map/all_gather | solution.py:109
  142.0 73.5 %all-gather.12.cloned.1.call-start = ((), (), s32[]{:S(2)}) async-start(), calls=%async_computation.1 | async-start | bytes 5242880 | tf_op jit(solution)/shard_map/all_gather | solution.py:109
  180.8 74.5 %all-gather.14.cloned.1.call-start = ((), (), s32[]{:S(2)}) async-start(), calls=%async_computation.2 | async-start | bytes 5242880 | tf_op jit(solution)/shard_map/all_gather | solution.py:109
  218.4 1.0 copy-start.2
  220.7 124.6 %all-gather.16.cloned.1.call-start = ((), (), s32[]{:S(2)}) async-start(), calls=%async_computation.3 | async-start | bytes 5242880 | tf_op jit(solution)/shard_map/all_gather | solution.py:109
  222.1 39.9 %copy-start.13 = (u32[32]{0:T(128)S(1)}, u32[32]{0:T(128)}, u32[]{:S(2)}) copy-start(u32[32]{0:T(128)} %constant.105) | copy-start | bytes 388
  222.1 51.1 %copy-start.9 = (f32[4,1]{0,1:T(1,128)S(1)}, f32[4,1]{0,1:T(1,128)}, u32[]{:S(2)}) copy-start(f32[4,1]{0,1:T(1,128)} %param.23) | copy-start | bytes 52
  258.3 1.0 copy-start.3
  335.9 6.1 %copy-start.12 = (bf16[4,1,128]{2,0,1:T(4,128)(2,1)S(1)}, bf16[4,1,128]{2,0,1:T(4,128)(2,1)}, u32[]{:S(2)}) copy-start(bf16[4,1,128]{2,0,1:T(4,128)(2,1)} %param.21) | copy-start | bytes 3076
  339.6 5.0 %copy-start.4 = (f32[32,64,128]{2,1,0:T(8,128)S(1)}, f32[32,64,128]{2,1,0:T(8,128)}, u32[]{:S(2)}) copy-start(f32[32,64,128]{2,1,0:T(8,128)} %copy-done.3) | copy-start | bytes 3145732
Sparse Core Ops, SparseCore 0:
  12.4 81.9 all-gather.17
  107.3 32.2 all-gather.9
  142.1 34.4 all-gather.19
  181.0 34.4 all-gather.11
  220.8 34.4 all-gather.13
  260.8 34.6 all-gather.15
where the time goes:
time: 362 us; the launch traced here: 358 us
  waiting for transfers between devices  204 us (56%)
  other arithmetic  47.2 us (13%)
  blocking collectives  40 us (11%)
  between operations  29.5 us (8%)
  local copies, waits for them, and re-layouts  25.3 us (7%)
  matrix products  9.31 us (3%)
    all_gather x4, waiting for transfers between devices, on_device(): lax.all_gather(state_now[None], 'beam', axis=0, tiled=True)  98.2 us
    all_gather x1, waiting for transfers between devices, on_device(): lax.all_gather(segment_finish[None], 'seq', axis=0, tiled=True)  73 us
    all_gather x1, waiting for transfers between devices, on_device(): every_head = lax.all_gather(full_block, 'beam', axis=0, tiled=True)  32.4 us
    unnamed x4, blocking collectives  24.3 us
    unnamed x46, local copies, waits for them, and re-layouts  16.5 us
    reduce_sum x4, other arithmetic, on_device(): jnp.sum(picked[:, None, None, None] * pieces[0], axis=0, keepdims=True)  11.5 us
    all_gather x1, blocking collectives, on_device(): lax.all_gather(total_decay[None], 'seq', axis=0, tiled=True)  9.08 us
  transfers between devices with their start and end apart: 6, of which 5 were waited for; matrix products, arithmetic and copies ran while one was open for 12% of the time, Pallas kernels for 0%

commit v1 on v0

v1 whole, which is shorter than its diff:
```python
import functools
import math

import jax
import jax.numpy as jnp
from jax import lax
from jax.experimental import pallas as pl
from jax.experimental.pallas import tpu as pltpu
from jax.sharding import PartitionSpec as P

P_SIZE = 64
LANES = 128
PAIR = LANES // P_SIZE
ROWS = 8
LAG = 2
LOG2E = math.log2(math.e)
MESH = pl.DeviceIdType.MESH
F32 = jnp.float32
BF16 = jnp.bfloat16


def split3(x):
    first = x.astype(BF16)
    rest = x - first.astype(F32)
    second = rest.astype(BF16)
    return first, second, (rest - second.astype(F32)).astype(BF16)


def mm(a, b):
    return jnp.dot(a, b, preferred_element_type=F32)


def mm_first(a, b):
    return lax.dot_general(a, b, (((0,), (0,)), ((), ())), preferred_element_type=F32)


def kernel(
    ns,
    nb,
    x_ref,
    keys_ref,
    queries_ref,
    decay_ref,
    sv_ref,
    sk_ref,
    sq_ref,
    sd_ref,
    lp_ref,
    par_ref,
    fin_ref,
    len_ref,
    score_ref,
    out_ref,
    so_ref,
    rank_ref,
    beam_ref,
    sums_ref,
    keys_t,
    scores,
    own,
    inner_ref,
    up_recv,
    up_out,
    dn_recv,
    dn_out,
    final,
    vals,
    small,
    pad,
    dec_d,
    dec_add,
    dec_cv,
    dec_k,
    dec_q,
    up_ss,
    up_rs,
    dn_ss,
    dn_rs,
    f_ss,
    f_rs,
    v_ss,
    v_rs,
    m_ss,
    m_rs,
):
    g = lax.axis_index("groups")
    s = lax.axis_index("seq")
    b = lax.axis_index("beam")
    toks, width = x_ref.shape
    n = keys_ref.shape[1]
    chunks = width // LANES
    steps = sv_ref.shape[0]
    dwidth = sv_ref.shape[2]
    dheads = dwidth // P_SIZE
    dchunks = dwidth // LANES
    last = ns - 1

    barrier = pltpu.get_barrier_semaphore()

    def peer(i):
        return lax.rem(b + i, nb)

    @pl.when(s > 0)
    def _():
        pl.semaphore_signal(barrier, inc=1, device_id=(g, s - 1, b), device_id_type=MESH)

    @pl.when(s < last)
    def _():
        pl.semaphore_signal(barrier, inc=1, device_id=(g, s + 1, b), device_id_type=MESH)

    for i in range(1, nb):
        pl.semaphore_signal(barrier, inc=1, device_id=(g, s, peer(i)), device_id_type=MESH)

    def up_copy(src, k):
        return pltpu.make_async_remote_copy(
            src_ref=src,
            dst_ref=up_recv.at[k],
            send_sem=up_ss.at[k],
            recv_sem=up_rs.at[k],
            device_id=(g, lax.rem(s + 1, ns), b),
            device_id_type=MESH,
        )

    def dn_copy(src, k):
        return pltpu.make_async_remote_copy(
            src_ref=src,
            dst_ref=dn_recv.at[k],
            send_sem=dn_ss.at[k],
            recv_sem=dn_rs.at[k],
            device_id=(g, lax.rem(s + ns - 1, ns), b),
            device_id_type=MESH,
        )

    def f_copy(kk, i):
        return pltpu.make_async_remote_copy(
            src_ref=final.at[kk],
            dst_ref=final.at[kk],
            send_sem=f_ss.at[kk, i - 1],
            recv_sem=f_rs.at[kk],
            device_id=(g, s, peer(i)),
            device_id_type=MESH,
        )

    def v_copy(i):
        return pltpu.make_async_remote_copy(
            src_ref=vals.at[b],
            dst_ref=vals.at[b],
            send_sem=v_ss.at[i - 1],
            recv_sem=v_rs.at[i - 1],
            device_id=(g, s, peer(i)),
            device_id_type=MESH,
        )

    def m_copy(i):
        return pltpu.make_async_remote_copy(
            src_ref=small.at[b],
            dst_ref=small.at[b],
            send_sem=m_ss.at[i - 1],
            recv_sem=m_rs.at[i - 1],
            device_id=(g, s, peer(i)),
            device_id_type=MESH,
        )

    def target(k):
        return (b * chunks + k) // dchunks

    def place(k):
        return lax.rem(b * chunks + k, dchunks)

    row_id = lax.broadcasted_iota(jnp.int32, (toks, toks), 0)
    col_id = lax.broadcasted_iota(jnp.int32, (toks, toks), 1)
    upper = (row_id <= col_id).astype(F32).astype(BF16)
    parts = split3(decay_ref[...] * LOG2E)
    sums_ref[...] = sum(mm_first(part, upper) for part in reversed(parts))
    keys_t[...] = keys_ref[...].astype(F32).T.astype(BF16)

    left = lax.broadcasted_iota(jnp.int32, (1, LANES), 1) < P_SIZE

    def head_column(head):
        row = sums_ref[pl.ds(head, 1), :]
        return row, jnp.broadcast_to(row, (LANES, toks)).T

    def pair_columns(k):
        heads = [head_column(k * PAIR + j) for j in range(PAIR)]
        return heads, jnp.where(left, heads[0][1], heads[1][1])

    def lanes_of(k):
        return pl.ds(pl.multiple_of(k * LANES, LANES), LANES)

    def make_state(k, carry):
        _, column = pair_columns(k)
        end = column[toks - 1 : toks, :]
        scaled = (x_ref[:, lanes_of(k)].astype(F32) * jnp.exp2(end - column)).astype(BF16)
        own[k, 0:n, :] = mm(keys_t[...], scaled)
        own[k, n : n + ROWS, :] = jnp.broadcast_to(jnp.exp2(end), (ROWS, LANES))
        return carry

    live = (1 - fin_ref[...]).astype(F32)
    pad[...] = jnp.zeros_like(pad)
    pad[0:steps, 0:dheads] = sd_ref[:, 0, :] * live * LOG2E
    spread = (
        lax.broadcasted_iota(jnp.int32, (LANES, dwidth), 0)
        == lax.broadcasted_iota(jnp.int32, (LANES, dwidth), 1) // P_SIZE
    )
    spread = spread.astype(F32).astype(BF16)
    wide = sum(mm(part, spread) for part in reversed(split3(pad[...])))
    vals[b, 0:steps, :] = sv_ref[:, 0, :].astype(F32) * live
    vals[b, steps : 2 * steps, :] = wide[0:steps, :]
    small[b] = jnp.zeros(small.shape[1:], F32)
    small[b, 0:steps, :] = sk_ref[:, 0, :].astype(F32)
    shape = (steps, LANES)
    small[b, steps : 2 * steps, :] = jnp.broadcast_to(par_ref[...].astype(F32), shape)
    small[b, 2 * steps : 3 * steps, :] = jnp.broadcast_to(lp_ref[...] * live, shape)
    small[b, 3 * steps : 4 * steps, :] = jnp.broadcast_to(live, shape)
    small[b, 4 * steps : 4 * steps + 1, :] = jnp.broadcast_to(score_ref[...], (1, LANES))
    small[b, 4 * steps + 1 : 4 * steps + 2, :] = jnp.broadcast_to(len_ref[...].astype(F32), (1, LANES))

    make_state(0, 0)

    met = nb - 1 + jnp.where(s > 0, 1, 0) + jnp.where(s < last, 1, 0)
    pl.semaphore_wait(barrier, met)

    for i in range(1, nb):
        m_copy(i).start()
        v_copy(i).start()

    def first_sends(k):
        @pl.when((s == 0) & (s < last))
        def _():
            up_copy(own.at[k, pl.ds(0, n)], k).start()

        @pl.when((s == last) & (s > target(k)))
        def _():
            dn_copy(own.at[k], k).start()

    first_sends(0)

    def state_and_send(k, carry):
        make_state(k, 0)
        first_sends(k)
        return carry

    lax.fori_loop(1, chunks, state_and_send, 0)

    scores[...] = jnp.where(row_id >= col_id, mm(queries_ref[...], keys_t[...]), 0.0)

    for i in range(1, nb):
        m_copy(i).wait_recv()
        v_copy(i).wait_recv()

    dec_d[...] = jnp.zeros_like(dec_d)
    dec_add[...] = jnp.zeros_like(dec_add)
    dec_cv[...] = jnp.zeros_like(dec_cv)
    dec_k[...] = jnp.zeros_like(dec_k)
    dec_q[...] = jnp.zeros_like(dec_q)
    dec_q[0:steps, :] = sq_ref[:, 0, :].astype(F32)
    own_slot = [jnp.where(b == slot, jnp.ones((1, LANES), F32), 0.0) for slot in range(nb)]

    def pick(weights, ref, row):
        total = None
        for slot in range(nb):
            value = ref[slot, row : row + 1, :]
            weight = weights[slot] if value.shape[1] == LANES else weights[slot][:, 0:1]
            total = weight * value if total is None else total + weight * value
        return total

    for step in range(steps):
        chain = own_slot
        decay = jnp.zeros((1, dwidth), F32)
        added = jnp.zeros((1, dwidth), F32)
        query = dec_q[step : step + 1, :]
        for t in range(step, -1, -1):
            value = jnp.exp2(decay) * pick(chain, vals, t)
            key = pick(chain, small, t)
            added = added + jnp.sum(key * query, axis=1, keepdims=True) * value
            decay = decay + pick(chain, vals, steps + t)
            if step == steps - 1:
                high = value.astype(BF16).astype(F32)
                dec_cv[t : t + 1, :] = high
                dec_cv[ROWS + t : ROWS + t + 1, :] = value - high
                dec_k[t : t + 1, :] = key
                dec_k[ROWS + t : ROWS + t + 1, :] = key
            if t > 0:
                parent = pick(chain, small, steps + t)
                chain = [jnp.where(parent == float(slot), 1.0, 0.0) for slot in range(nb)]
        open_now = live[step : step + 1, :]
        dec_d[step : step + 1, :] = jnp.exp2(decay)
        dec_add[step : step + 1, :] = added * open_now

    score = [small[slot, 4 * steps : 4 * steps + 1, :] for slot in range(nb)]
    length = [small[slot, 4 * steps + 1 : 4 * steps + 2, :] for slot in range(nb)]
    for step in range(steps):
        new_score, new_length, normed = [], [], []
        for slot in range(nb):
            parent = small[slot, steps + step : steps + step + 1, :]
            picked_score, picked_length = score[0], length[0]
            for other in range(1, nb):
                picked_score = jnp.where(parent == float(other), score[other], picked_score)
                picked_length = jnp.where(parent == float(other), length[other], picked_length)
            new_score.append(picked_score + small[slot, 2 * steps + step : 2 * steps + step + 1, :])
            new_length.append(picked_length + small[slot, 3 * steps + step : 3 * steps + step + 1, :])
            normed.append(new_score[-1] / jnp.exp(0.6 * jnp.log((5.0 + new_length[-1]) / 6.0)))
        score, length = new_score, new_length
        best = functools.reduce(jnp.maximum, normed)
        mine = sum(own_slot[slot] * normed[slot] for slot in range(nb))
        rank_ref[step : step + 1, :] = (mine - best)[:, 0:1]

    def forward_down(k):
        dn_copy(dn_out.at[k], k).wait_recv()
        shrink = dn_recv[k, n : n + 1, :]
        dn_out[k, 0:n, :] = dn_recv[k, 0:n, :] + shrink * own[k, 0:n, :]
        dn_out[k, n : n + ROWS, :] = dn_recv[k, n : n + ROWS, :] * own[k, n : n + ROWS, :]
        dn_copy(dn_out.at[k], k).start()

    def finish(kk):
        at = lanes_of(kk)
        state = final[kk]
        read = mm(dec_q[...].astype(BF16), state.astype(BF16))
        keep = pad[:, 0:1]
        dec_add[:, at] = keep * (dec_d[:, at] * read) + dec_add[:, at]
        outer = mm_first(dec_cv[:, at].astype(BF16), dec_k[...].astype(BF16))
        rows = pl.ds(pl.multiple_of(kk * LANES, LANES), LANES)
        beam_ref[0, rows, :] = (state * dec_d[steps - 1 : steps, at]).T + outer

    def await_and_finish(kk):
        @pl.when(b != (s * dchunks) // chunks)
        def _():
            f_copy(kk, 1).wait_recv()

        finish(kk)

    pad[...] = jnp.zeros_like(pad)
    pad[0:steps, :] = jnp.broadcast_to(live, (steps, LANES))

    def body(k, carry):
        heads, column = pair_columns(k)
        values = x_ref[:, lanes_of(k)]
        for i in range(toks // LANES):
            at = slice(i * LANES, (i + 1) * LANES)
            until = (i + 1) * LANES
            made = []
            for row, col in heads:
                blocks = []
                for j in range(i + 1):
                    to = slice(j * LANES, (j + 1) * LANES)
                    gap = jnp.minimum(col[at, :] - row[:, to], 0.0)
                    blocks.append((scores[at, to] * jnp.exp2(gap)).astype(BF16))
                weights = blocks[0] if i == 0 else jnp.concatenate(blocks, axis=1)
                made.append(mm(weights, values[0:until, :]))
            inner_ref[at, :] = jnp.where(left, made[0], made[1])

        goes_down = (s > target(k)) & (s < last)

        @pl.when(goes_down & (2 * s >= ns))
        def _():
            forward_down(k)

        @pl.when(s == 0)
        def _():
            out_ref[:, lanes_of(k)] = inner_ref[...].astype(BF16)

        @pl.when(s > 0)
        def _():
            up_copy(up_out.at[k], k).wait_recv()

            @pl.when((s < last) | (s == target(k)))
            def _():
                up_out[k] = own[k, n : n + 1, :] * up_recv[k] + own[k, 0:n, :]

            @pl.when(s < last)
            def _():
                up_copy(up_out.at[k], k).start()

            carried = mm(queries_ref[...], up_recv[k].astype(BF16)) * jnp.exp2(column)
            out_ref[:, lanes_of(k)] = (inner_ref[...] + carried).astype(BF16)

        @pl.when(goes_down & (2 * s < ns))
        def _():
            forward_down(k)

        @pl.when(s == target(k))
        def _():
            kk = place(k)

            @pl.when(s == 0)
            def _():
                up_out[k] = own[k, 0:n, :]

            @pl.when(s < last)
            def _():
                dn_copy(dn_out.at[k], k).wait_recv()
                final[kk] = dn_recv[k, n : n + 1, :] * up_out[k] + dn_recv[k, 0:n, :]

            @pl.when(s == last)
            def _():
                final[kk] = up_out[k]

            for i in range(1, nb):
                f_copy(kk, i).start()

        if dchunks == chunks:

            @pl.when(k >= LAG)
            def _():
                await_and_finish(k - LAG)

        return carry

    lax.fori_loop(0, chunks, body, 0)

    def rest(kk, carry):
        await_and_finish(kk)
        return carry

    lax.fori_loop(max(chunks - LAG, 0) if dchunks == chunks else 0, dchunks, rest, 0)
    for step in range(steps):
        so_ref[step] = dec_add[step : step + 1, :].astype(BF16)

    for i in range(1, nb):
        m_copy(i).wait_send()
        v_copy(i).wait_send()

    def drain(k, carry):
        @pl.when(s < last)
        def _():
            up_copy(up_out.at[k], k).wait_send()

        @pl.when(s > target(k))
        def _():
            dn_copy(dn_out.at[k], k).wait_send()

        @pl.when(s == target(k))
        def _():
            for i in range(1, nb):
                f_copy(place(k), i).wait_send()

        return carry

    lax.fori_loop(0, chunks, drain, 0)


def on_device(ns, nb, *args):
    x, keys, queries, decay, sv, sk, sq, sd, lp, par, fin, lens, score = args
    toks, width = x.shape
    n = keys.shape[1]
    heads = decay.shape[1]
    steps, _, dwidth = sv.shape
    chunks, dchunks = width // LANES, dwidth // LANES
    small_rows = -(-(4 * steps + 2) // ROWS) * ROWS
    dma = pltpu.SemaphoreType.DMA
    spec = pl.BlockSpec(memory_space=pltpu.VMEM)
    peers = max(nb - 1, 1)
    return pl.pallas_call(
        functools.partial(kernel, ns, nb),
        out_shape=(
            jax.ShapeDtypeStruct((toks, width), BF16),
            jax.ShapeDtypeStruct((steps, 1, dwidth), BF16),
            jax.ShapeDtypeStruct((steps, 1), F32),
            jax.ShapeDtypeStruct((1, dwidth, n), F32),
        ),
        in_specs=[spec] * 13,
        out_specs=(spec,) * 4,
        scratch_shapes=[
            pltpu.VMEM((heads, toks), F32),
            pltpu.VMEM((n, toks), BF16),
            pltpu.VMEM((toks, toks), F32),
            pltpu.VMEM((chunks, n + ROWS, LANES), F32),
            pltpu.VMEM((toks, LANES), F32),
            pltpu.VMEM((chunks, n, LANES), F32),
            pltpu.VMEM((chunks, n, LANES), F32),
            pltpu.VMEM((chunks, n + ROWS, LANES), F32),
            pltpu.VMEM((chunks, n + ROWS, LANES), F32),
            pltpu.VMEM((dchunks, n, LANES), F32),
            pltpu.VMEM((nb, 2 * steps, dwidth), F32),
            pltpu.VMEM((nb, small_rows, LANES), F32),
            pltpu.VMEM((ROWS, LANES), F32),
            pltpu.VMEM((ROWS, dwidth), F32),
            pltpu.VMEM((ROWS, dwidth), F32),
            pltpu.VMEM((2 * ROWS, dwidth), F32),
            pltpu.VMEM((2 * ROWS, n), F32),
            pltpu.VMEM((ROWS, n), F32),
            dma((chunks,)),
            dma((chunks,)),
            dma((chunks,)),
            dma((chunks,)),
            dma((dchunks, peers)),
            dma((dchunks,)),
            dma((peers,)),
            dma((peers,)),
            dma((peers,)),
            dma((peers,)),
        ],
        compiler_params=pltpu.CompilerParams(
            collective_id=0, has_side_effects=True, vmem_limit_bytes=40 * 1024 * 1024
        ),
    )(x, keys, queries, decay, sv, sk, sq, sd, lp, par, fin, lens.reshape(1, 1), score.reshape(1, 1))


def solution(mesh):
    return jax.shard_map(
        functools.partial(on_device, mesh.shape["seq"], mesh.shape["beam"]),
        mesh=mesh,
        in_specs=(
            P(("groups", "seq"), "beam"),
            P(("groups", "seq"), None),
            P(("groups", "seq"), None),
            P(("groups", "seq"), "beam"),
            P("groups", "beam", "seq"),
            P("groups", "beam", None),
            P("groups", "beam", None),
            P("groups", "beam", "seq"),
            P("groups", "beam"),
            P("groups", "beam"),
            P("groups", "beam"),
            P(("groups", "beam")),
            P(("groups", "beam")),
        ),
        out_specs=(
            P(("groups", "seq"), "beam"),
            P("groups", "beam", "seq"),
            P("groups", "beam"),
            P(("groups", "beam"), "seq", None),
        ),
        check_vma=False,
    )
```

time: 362 us -> 90.1 us (0.25); the launches traced: 358 us -> 89.7 us
  waiting for transfers between devices: 204 us -> 0 us
  Pallas kernels: 0 us -> 79.4 us
  other arithmetic: 47.2 us -> 0 us
  blocking collectives: 40 us -> 0 us
  between operations: 29.5 us -> 2.03 us
  local copies, waits for them, and re-layouts: 25.3 us -> 8.22 us
  matrix products: 9.31 us -> 0 us
    all_gather x6 -> x0, waiting for transfers between devices: 204 us -> none  [the longest x4 98.2 us: on_device(): lax.all_gather(state_now[None], 'beam', axis=0, tiled=True)]
    pallas_call x0 -> x1, Pallas kernels: none -> 79.4 us  [on_device(): pl.pallas_call(functools.partial(kernel, ns, nb), out_shape=(jax.ShapeDty...]
    unnamed x4 -> x0, blocking collectives: 24.3 us -> none
    reduce_sum x11 -> x0, other arithmetic: 20.3 us -> none  [the longest x4 11.5 us: on_device(): jnp.sum(picked[:, None, None, None] * pieces[0], axis=0, keepdims=True)]
    unnamed x46 -> x23, local copies, waits for them, and re-layouts: 16.5 us -> 7 us
    dot_general x8 -> x0, matrix products: 9.31 us -> none  [the longest x1 3.71 us: within(): jnp.einsum('ijh,jhp->ihp', weights, values_one, preferred_element_type=jn...]
    add x7 -> x0, other arithmetic: 9.21 us -> none  [the longest x4 5.64 us: collect(): running = decay_one[:, None, None] * running + state_one]
    all_gather x1 -> x0, blocking collectives: 9.08 us -> none  [on_device(): lax.all_gather(total_decay[None], 'seq', axis=0, tiled=True)]
  transfers between devices with their start and end apart: 6 -> 0, of which waited for: 5 -> 0; matrix products, arithmetic and copies ran while one was open for 12% -> 0% of each run, Pallas kernels for 0% -> 0%
where the time goes in v1:
time: 90.1 us; the launch traced here: 89.7 us
  Pallas kernels  79.4 us (88%)
  local copies, waits for them, and re-layouts  8.22 us (9%)
  between operations  2.03 us (2%)
    pallas_call x1, Pallas kernels, on_device(): pl.pallas_call(functools.partial(kernel, ns, nb), out_shape=(jax.ShapeDty...  79.4 us
    unnamed x23, local copies, waits for them, and re-layouts  7 us

profile of v1, /device:TPU:3, one launch (start us, length us, event | category | flops | bytes accessed | tf_op | source)
XLA Modules:
  0.0 89.7 jit_solution(785909627323904099)
XLA Ops:
  0.6 0.0 copy-start.5
  1.3 0.0 copy-start.6
  2.0 0.0 copy-start.4
  2.0 0.7 copy.19.sk_ref
  2.7 0.7 copy.20.sq_ref
  3.4 0.7 copy.21.lp_ref
  4.1 0.7 copy.22.par_ref
  4.8 0.0 copy-done.6
  4.8 0.1 copy.23.fin_ref
  4.9 0.0 copy-done.5
  5.0 0.0 copy-done.4
  5.0 0.0 copy-start.1
  5.0 0.0 copy-start.2
  5.0 0.0 copy-start.3
  5.0 0.1 copy.17.decay_ref
  5.1 0.7 copy-done.1
  5.8 0.0 copy-done.2
  5.8 0.0 copy-done.3
  5.9 0.0 copy-start
  5.9 1.2 %copy-done = bf16[256,2048]{1,0:T(8,128)(2,1)S(1)} copy-done((bf16[256,2048]{1,0:T(8,128)(2,1)S(1)}, bf16[256,2048]{1,0:T(8,128)(2,1)}, u32[]{:S(2)}) %copy-start) | copy-done | bytes 1048600
  7.1 79.4 %shard_map.156 = (bf16[256,2048]{1,0:T(8,128)(2,1)S(1)}, bf16[4,1,2048]{2,1,0:T(2,128)(2,1)S(1)}, f32[4,1]{1,0:T(4,128)S(1)}, f32[1,2048,128]{2,1,0:T(8,128)S(1)}) custom-call(bf16[256,2048]{1,0:T(8,128)(2,1)S(1)} %copy-done, bf16[256,128]{1,0:T(8,128)(2,1)S(1)} %copy-done.1, bf16[256,128]{1,0:T(8,128)(2,1)S(1)} %copy-done.2, f32[256,32]{1,0:T(8,128)S(1)} %copy.17.decay_ref, ...), custom_call_target="tpu_custom_call" | custom-call | tf_op jit(solution)/shard_map/pallas_call | solution.py:453
  86.5 0.6 copy.25
  87.1 0.6 copy.24
  87.8 1.0 %copy.30 = bf16[256,2048]{1,0:T(8,128)(2,1)} copy(bf16[256,2048]{1,0:T(8,128)(2,1)S(1)} %get-tuple-element.12) | data formatting | bytes 2097152
  88.7 1.0 %copy.31 = f32[1,2048,128]{2,1,0:T(8,128)} copy(f32[1,2048,128]{2,1,0:T(8,128)S(1)} %get-tuple-element.15) | data formatting | bytes 2097152
  (1 shorter events, 0.0 us)
Async XLA Ops:
  0.6 4.3 %copy-start.5 = (bf16[4,1,2048]{2,0,1:T(4,128)(2,1)S(1)}, bf16[4,1,2048]{2,0,1:T(4,128)(2,1)}, u32[]{:S(2)}) copy-start(bf16[4,1,2048]{2,0,1:T(4,128)(2,1)} %param.17) | copy-start | bytes 49156
  1.3 3.5 %copy-start.6 = (s32[4,1]{0,1:T(1,128)S(1)}, s32[4,1]{0,1:T(1,128)}, u32[]{:S(2)}) copy-start(s32[4,1]{0,1:T(1,128)} %param.23) | copy-start | bytes 52
  2.0 3.0 %copy-start.4 = (f32[256,32]{0,1:T(8,128)S(1)}, f32[256,32]{0,1:T(8,128)}, u32[]{:S(2)}) copy-start(f32[256,32]{0,1:T(8,128)} %param.16) | copy-start | bytes 98308
  5.0 0.8 copy-start.1
  5.0 0.9 copy-start.2
  5.0 0.9 copy-start.3
  5.9 1.2 %copy-start = (bf16[256,2048]{1,0:T(8,128)(2,1)S(1)}, bf16[256,2048]{1,0:T(8,128)(2,1)}, u32[]{:S(2)}) copy-start(bf16[256,2048]{1,0:T(8,128)(2,1)} %x_ref.1) | copy-start | bytes 3145732

commit v2 on v1

--- a/solution.py
+++ b/solution.py
@@ -12,7 +12,9 @@
 LANES = 128
 PAIR = LANES // P_SIZE
 ROWS = 8
-LAG = 2
+HOP = 2
+SHARE = 2
+START = 2
 LOG2E = math.log2(math.e)
 MESH = pl.DeviceIdType.MESH
 F32 = jnp.float32
@@ -55,6 +57,8 @@
     rank_ref,
     beam_ref,
     sums_ref,
+    cols,
+    grown,
     keys_t,
     scores,
     own,
@@ -89,8 +93,7 @@
     toks, width = x_ref.shape
     n = keys_ref.shape[1]
     chunks = width // LANES
-    steps = sv_ref.shape[0]
-    dwidth = sv_ref.shape[2]
+    _, steps, dwidth = sv_ref.shape
     dheads = dwidth // P_SIZE
     dchunks = dwidth // LANES
     last = ns - 1
@@ -171,49 +174,56 @@
     col_id = lax.broadcasted_iota(jnp.int32, (toks, toks), 1)
     upper = (row_id <= col_id).astype(F32).astype(BF16)
     parts = split3(decay_ref[...] * LOG2E)
-    sums_ref[...] = sum(mm_first(part, upper) for part in reversed(parts))
+    sums_ref[...] = sum(mm(part, upper) for part in reversed(parts))
     keys_t[...] = keys_ref[...].astype(F32).T.astype(BF16)
 
     left = lax.broadcasted_iota(jnp.int32, (1, LANES), 1) < P_SIZE
 
-    def head_column(head):
+    def make_column(head):
         row = sums_ref[pl.ds(head, 1), :]
-        return row, jnp.broadcast_to(row, (LANES, toks)).T
-
-    def pair_columns(k):
-        heads = [head_column(k * PAIR + j) for j in range(PAIR)]
-        return heads, jnp.where(left, heads[0][1], heads[1][1])
+        column = jnp.broadcast_to(row, (LANES, toks)).T
+        cols[head] = column
+        return column
 
     def lanes_of(k):
         return pl.ds(pl.multiple_of(k * LANES, LANES), LANES)
 
     def make_state(k, carry):
-        _, column = pair_columns(k)
+        column = jnp.where(left, make_column(k * PAIR), make_column(k * PAIR + 1))
         end = column[toks - 1 : toks, :]
         scaled = (x_ref[:, lanes_of(k)].astype(F32) * jnp.exp2(end - column)).astype(BF16)
         own[k, 0:n, :] = mm(keys_t[...], scaled)
+        grown[k] = jnp.exp2(column)
         own[k, n : n + ROWS, :] = jnp.broadcast_to(jnp.exp2(end), (ROWS, LANES))
         return carry
 
-    live = (1 - fin_ref[...]).astype(F32)
+    def column_of(row):
+        row = row.astype(F32)
+        pad[...] = jnp.zeros_like(pad)
+        for step in range(steps):
+            pad[step : step + 1, :] = jnp.broadcast_to(row[:, step : step + 1], (1, LANES))
+        return pad[0:steps, :]
+
+    live = 1.0 - column_of(fin_ref[...])
+    chance = column_of(lp_ref[...]) * live
+    parent_of = column_of(par_ref[...])
     pad[...] = jnp.zeros_like(pad)
-    pad[0:steps, 0:dheads] = sd_ref[:, 0, :] * live * LOG2E
+    pad[0:steps, 0:dheads] = sd_ref[:, 0, :] * live[:, 0:1] * LOG2E
     spread = (
         lax.broadcasted_iota(jnp.int32, (LANES, dwidth), 0)
         == lax.broadcasted_iota(jnp.int32, (LANES, dwidth), 1) // P_SIZE
     )
     spread = spread.astype(F32).astype(BF16)
     wide = sum(mm(part, spread) for part in reversed(split3(pad[...])))
-    vals[b, 0:steps, :] = sv_ref[:, 0, :].astype(F32) * live
+    vals[b, 0:steps, :] = sv_ref[0].astype(F32) * live[:, 0:1]
     vals[b, steps : 2 * steps, :] = wide[0:steps, :]
     small[b] = jnp.zeros(small.shape[1:], F32)
-    small[b, 0:steps, :] = sk_ref[:, 0, :].astype(F32)
-    shape = (steps, LANES)
-    small[b, steps : 2 * steps, :] = jnp.broadcast_to(par_ref[...].astype(F32), shape)
-    small[b, 2 * steps : 3 * steps, :] = jnp.broadcast_to(lp_ref[...] * live, shape)
-    small[b, 3 * steps : 4 * steps, :] = jnp.broadcast_to(live, shape)
-    small[b, 4 * steps : 4 * steps + 1, :] = jnp.broadcast_to(score_ref[...], (1, LANES))
-    small[b, 4 * steps + 1 : 4 * steps + 2, :] = jnp.broadcast_to(len_ref[...].astype(F32), (1, LANES))
+    small[b, 0:steps, :] = sk_ref[0].astype(F32)
+    small[b, steps : 2 * steps, :] = parent_of
+    small[b, 2 * steps : 3 * steps, :] = chance
+    small[b, 3 * steps : 4 * steps, :] = live
+    small[b, 4 * steps : 4 * steps + 1, :] = jnp.full((1, LANES), score_ref[0], F32)
+    small[b, 4 * steps + 1 : 4 * steps + 2, :] = jnp.full((1, LANES), len_ref[0], jnp.int32).astype(F32)
 
     make_state(0, 0)
 
@@ -244,16 +254,14 @@
 
     scores[...] = jnp.where(row_id >= col_id, mm(queries_ref[...], keys_t[...]), 0.0)
 
-    for i in range(1, nb):
-        m_copy(i).wait_recv()
-        v_copy(i).wait_recv()
-
+    pad[...] = jnp.zeros_like(pad)
+    pad[0:steps, :] = live
     dec_d[...] = jnp.zeros_like(dec_d)
     dec_add[...] = jnp.zeros_like(dec_add)
     dec_cv[...] = jnp.zeros_like(dec_cv)
     dec_k[...] = jnp.zeros_like(dec_k)
     dec_q[...] = jnp.zeros_like(dec_q)
-    dec_q[0:steps, :] = sq_ref[:, 0, :].astype(F32)
+    dec_q[0:steps, :] = sq_ref[0].astype(F32)
     own_slot = [jnp.where(b == slot, jnp.ones((1, LANES), F32), 0.0) for slot in range(nb)]
 
     def pick(weights, ref, row):
@@ -264,7 +272,7 @@
             total = weight * value if total is None else total + weight * value
         return total
 
-    for step in range(steps):
+    def prepare(step):
         chain = own_slot
         decay = jnp.zeros((1, dwidth), F32)
         added = jnp.zeros((1, dwidth), F32)
@@ -283,27 +291,28 @@
             if t > 0:
                 parent = pick(chain, small, steps + t)
                 chain = [jnp.where(parent == float(slot), 1.0, 0.0) for slot in range(nb)]
-        open_now = live[step : step + 1, :]
+        open_now = pad[step : step + 1, 0:1]
         dec_d[step : step + 1, :] = jnp.exp2(decay)
         dec_add[step : step + 1, :] = added * open_now
 
-    score = [small[slot, 4 * steps : 4 * steps + 1, :] for slot in range(nb)]
-    length = [small[slot, 4 * steps + 1 : 4 * steps + 2, :] for slot in range(nb)]
-    for step in range(steps):
-        new_score, new_length, normed = [], [], []
-        for slot in range(nb):
-            parent = small[slot, steps + step : steps + step + 1, :]
-            picked_score, picked_length = score[0], length[0]
-            for other in range(1, nb):
-                picked_score = jnp.where(parent == float(other), score[other], picked_score)
-                picked_length = jnp.where(parent == float(other), length[other], picked_length)
-            new_score.append(picked_score + small[slot, 2 * steps + step : 2 * steps + step + 1, :])
-            new_length.append(picked_length + small[slot, 3 * steps + step : 3 * steps + step + 1, :])
-            normed.append(new_score[-1] / jnp.exp(0.6 * jnp.log((5.0 + new_length[-1]) / 6.0)))
-        score, length = new_score, new_length
-        best = functools.reduce(jnp.maximum, normed)
-        mine = sum(own_slot[slot] * normed[slot] for slot in range(nb))
-        rank_ref[step : step + 1, :] = (mine - best)[:, 0:1]
+    def rank_slots():
+        score = [small[slot, 4 * steps : 4 * steps + 1, :] for slot in range(nb)]
+        length = [small[slot, 4 * steps + 1 : 4 * steps + 2, :] for slot in range(nb)]
+        for step in range(steps):
+            new_score, new_length, normed = [], [], []
+            for slot in range(nb):
+                parent = small[slot, steps + step : steps + step + 1, :]
+                picked_score, picked_length = score[0], length[0]
+                for other in range(1, nb):
+                    picked_score = jnp.where(parent == float(other), score[other], picked_score)
+                    picked_length = jnp.where(parent == float(other), length[other], picked_length)
+                new_score.append(picked_score + small[slot, 2 * steps + step : 2 * steps + step + 1, :])
+                new_length.append(picked_length + small[slot, 3 * steps + step : 3 * steps + step + 1, :])
+                normed.append(new_score[-1] / jnp.exp(0.6 * jnp.log((5.0 + new_length[-1]) / 6.0)))
+            score, length = new_score, new_length
+            best = functools.reduce(jnp.maximum, normed)
+            mine = sum(own_slot[slot] * normed[slot] for slot in range(nb))
+            rank_ref[:, step : step + 1] = (mine - best)[:, 0:1]
 
     def forward_down(k):
         dn_copy(dn_out.at[k], k).wait_recv()
@@ -329,92 +338,109 @@
 
         finish(kk)
 
-    pad[...] = jnp.zeros_like(pad)
-    pad[0:steps, :] = jnp.broadcast_to(live, (steps, LANES))
-
-    def body(k, carry):
-        heads, column = pair_columns(k)
+    up_lag = s * HOP
+    dn_lag = (last - s) * HOP
+    own_lag = jnp.maximum(jnp.maximum(up_lag, dn_lag), START + steps - SHARE)
+    first = lax.rem(s * dchunks, chunks)
+    slots = chunks + max(last * HOP, START + steps - SHARE) + SHARE
+
+    def inside(k):
+        return (k >= 0) & (k < chunks)
+
+    def make_inner(k):
         values = x_ref[:, lanes_of(k)]
         for i in range(toks // LANES):
             at = slice(i * LANES, (i + 1) * LANES)
             until = (i + 1) * LANES
             made = []
-            for row, col in heads:
+            for j in range(PAIR):
+                row = sums_ref[pl.ds(k * PAIR + j, 1), :]
+                col = cols[k * PAIR + j, at, :]
                 blocks = []
-                for j in range(i + 1):
-                    to = slice(j * LANES, (j + 1) * LANES)
-                    gap = jnp.minimum(col[at, :] - row[:, to], 0.0)
+                for other in range(i + 1):
+                    to = slice(other * LANES, (other + 1) * LANES)
+                    gap = jnp.minimum(col - row[:, to], 0.0)
                     blocks.append((scores[at, to] * jnp.exp2(gap)).astype(BF16))
                 weights = blocks[0] if i == 0 else jnp.concatenate(blocks, axis=1)
                 made.append(mm(weights, values[0:until, :]))
-            inner_ref[at, :] = jnp.where(left, made[0], made[1])
-
-        goes_down = (s > target(k)) & (s < last)
-
-        @pl.when(goes_down & (2 * s >= ns))
-        def _():
-            forward_down(k)
-
+            inner_ref[k, at, :] = jnp.where(left, made[0], made[1])
+
+    def take_up(k):
         @pl.when(s == 0)
         def _():
-            out_ref[:, lanes_of(k)] = inner_ref[...].astype(BF16)
+            up_out[k] = own[k, 0:n, :]
+            out_ref[:, lanes_of(k)] = inner_ref[k].astype(BF16)
 
         @pl.when(s > 0)
         def _():
             up_copy(up_out.at[k], k).wait_recv()
-
-            @pl.when((s < last) | (s == target(k)))
-            def _():
-                up_out[k] = own[k, n : n + 1, :] * up_recv[k] + own[k, 0:n, :]
+            up_out[k] = own[k, n : n + 1, :] * up_recv[k] + own[k, 0:n, :]
 
             @pl.when(s < last)
             def _():
                 up_copy(up_out.at[k], k).start()
 
-            carried = mm(queries_ref[...], up_recv[k].astype(BF16)) * jnp.exp2(column)
-            out_ref[:, lanes_of(k)] = (inner_ref[...] + carried).astype(BF16)
-
-        @pl.when(goes_down & (2 * s < ns))
-        def _():
-            forward_down(k)
-
-        @pl.when(s == target(k))
-        def _():
-            kk = place(k)
-
-            @pl.when(s == 0)
+            carried = mm(queries_ref[...], up_recv[k].astype(BF16)) * grown[k]
+            out_ref[:, lanes_of(k)] = (inner_ref[k] + carried).astype(BF16)
+
+    def share_final(k):
+        kk = place(k)
+
+        @pl.when(s < last)
+        def _():
+            dn_copy(dn_out.at[k], k).wait_recv()
+            final[kk] = dn_recv[k, n : n + 1, :] * up_out[k] + dn_recv[k, 0:n, :]
+
+        @pl.when(s == last)
+        def _():
+            final[kk] = up_out[k]
+
+        for i in range(1, nb):
+            f_copy(kk, i).start()
+
+    def body(slot, carry):
+        for step in range(steps):
+
+            @pl.when(slot == START + step)
             def _():
-                up_out[k] = own[k, 0:n, :]
-
-            @pl.when(s < last)
-            def _():
-                dn_copy(dn_out.at[k], k).wait_recv()
-                final[kk] = dn_recv[k, n : n + 1, :] * up_out[k] + dn_recv[k, 0:n, :]
-
-            @pl.when(s == last)
-            def _():
-                final[kk] = up_out[k]
-
-            for i in range(1, nb):
-                f_copy(kk, i).start()
-
-        if dchunks == chunks:
-
-            @pl.when(k >= LAG)
-            def _():
-                await_and_finish(k - LAG)
+                if step == 0:
+                    for i in range(1, nb):
+                        m_copy(i).wait_recv()
+                        v_copy(i).wait_recv()
+                prepare(step)
+
+        @pl.when(slot < chunks)
+        def _():
+            make_inner(slot)
+
+        @pl.when(inside(slot - up_lag))
+        def _():
+            take_up(slot - up_lag)
+
+        down = slot - dn_lag
+
+        @pl.when(inside(down) & (s > target(down)) & (s < last))
+        def _():
+            forward_down(down)
+
+        at_end = slot - own_lag
+
+        @pl.when(inside(at_end) & (s == target(at_end)))
+        def _():
+            share_final(at_end)
+
+        kk = slot - own_lag - SHARE - first
+
+        @pl.when((kk >= 0) & (kk < dchunks))
+        def _():
+            await_and_finish(kk)
 
         return carry
 
-    lax.fori_loop(0, chunks, body, 0)
-
-    def rest(kk, carry):
-        await_and_finish(kk)
-        return carry
-
-    lax.fori_loop(max(chunks - LAG, 0) if dchunks == chunks else 0, dchunks, rest, 0)
+    lax.fori_loop(0, slots, body, 0)
+    rank_slots()
     for step in range(steps):
-        so_ref[step] = dec_add[step : step + 1, :].astype(BF16)
+        so_ref[:, step : step + 1, :] = dec_add[step : step + 1, :].astype(BF16)[None]
 
     for i in range(1, nb):
         m_copy(i).wait_send()
@@ -449,23 +475,27 @@
     small_rows = -(-(4 * steps + 2) // ROWS) * ROWS
     dma = pltpu.SemaphoreType.DMA
     spec = pl.BlockSpec(memory_space=pltpu.VMEM)
+    scalar = pl.BlockSpec(memory_space=pltpu.SMEM)
     peers = max(nb - 1, 1)
-    return pl.pallas_call(
+    turn = lambda a: jnp.transpose(a, (1, 0, 2))
+    prompt, step_out, ranked, states = pl.pallas_call(
         functools.partial(kernel, ns, nb),
         out_shape=(
             jax.ShapeDtypeStruct((toks, width), BF16),
-            jax.ShapeDtypeStruct((steps, 1, dwidth), BF16),
-            jax.ShapeDtypeStruct((steps, 1), F32),
+            jax.ShapeDtypeStruct((1, steps, dwidth), BF16),
+            jax.ShapeDtypeStruct((1, steps), F32),
             jax.ShapeDtypeStruct((1, dwidth, n), F32),
         ),
-        in_specs=[spec] * 13,
+        in_specs=[spec] * 11 + [scalar] * 2,
         out_specs=(spec,) * 4,
         scratch_shapes=[
             pltpu.VMEM((heads, toks), F32),
+            pltpu.VMEM((heads, toks, LANES), F32),
+            pltpu.VMEM((chunks, toks, LANES), F32),
             pltpu.VMEM((n, toks), BF16),
             pltpu.VMEM((toks, toks), F32),
             pltpu.VMEM((chunks, n + ROWS, LANES), F32),
-            pltpu.VMEM((toks, LANES), F32),
+            pltpu.VMEM((chunks, toks, LANES), F32),
             pltpu.VMEM((chunks, n, LANES), F32),
             pltpu.VMEM((chunks, n, LANES), F32),
             pltpu.VMEM((chunks, n + ROWS, LANES), F32),
@@ -493,7 +523,8 @@
         compiler_params=pltpu.CompilerParams(
             collective_id=0, has_side_effects=True, vmem_limit_bytes=40 * 1024 * 1024
         ),
-    )(x, keys, queries, decay, sv, sk, sq, sd, lp, par, fin, lens.reshape(1, 1), score.reshape(1, 1))
+    )(x, keys, queries, decay.T, turn(sv), turn(sk), turn(sq), sd, lp.T, par.T, fin.T, lens, score)
+    return prompt, turn(step_out), ranked.T, states
 
 
 def solution(mesh):

time: 90.1 us -> 58 us (0.64)
  Pallas kernels: 79.4 us -> 44.9 us
  local copies, waits for them, and re-layouts: 8.22 us -> 10.7 us
    pallas_call x1, Pallas kernels: 79.4 us -> 44.9 us  [on_device(): pl.pallas_call(functools.partial(kernel, ns, nb), out_shape=(jax.ShapeDty...]
    unnamed x23 -> x26, local copies, waits for them, and re-layouts: 7 us -> 10.7 us
    pallas_call x2 -> x0, local copies, waits for them, and re-layouts: 1.22 us -> none  [on_device(): pl.pallas_call(functools.partial(kernel, ns, nb), out_shape=(jax.ShapeDty...]
where the time goes in v2:
time: 58 us; the launch traced here: 57.6 us
  Pallas kernels  44.9 us (77%)
  local copies, waits for them, and re-layouts  10.7 us (18%)
  between operations  1.98 us (3%)
    pallas_call x1, Pallas kernels, on_device(): pl.pallas_call(functools.partial(kernel, ns, nb), out_shape=(jax.ShapeDty...  44.9 us
    unnamed x26, local copies, waits for them, and re-layouts  10.7 us

profile of v2, /device:TPU:3, one launch (start us, length us, event | category | flops | bytes accessed | tf_op | source)
XLA Modules:
  0.0 57.6 jit_solution(1158940649681837360)
XLA Ops:
  0.6 0.0 copy-start.4
  1.9 0.0 copy-start.6
  2.0 0.0 copy-done.4
  2.0 0.7 %copy-done.6 = bf16[4,1,128]{2,0,1:T(4,128)(2,1)S(1)} copy-done((bf16[4,1,128]{2,0,1:T(4,128)(2,1)S(1)}, bf16[4,1,128]{2,0,1:T(4,128)(2,1)}, u32[]{:S(2)}) %copy-start.6) | copy-done | bytes 1048
  2.6 0.0 copy-start
  2.6 1.2 %copy-done = bf16[256,2048]{1,0:T(8,128)(2,1)S(1)} copy-done((bf16[256,2048]{1,0:T(8,128)(2,1)S(1)}, bf16[256,2048]{1,0:T(8,128)(2,1)}, u32[]{:S(2)}) %copy-start) | copy-done | bytes 1048600
  3.9 0.0 copy-start.1
  3.9 0.8 %copy-done.1 = bf16[256,128]{1,0:T(8,128)(2,1)S(1)} copy-done((bf16[256,128]{1,0:T(8,128)(2,1)S(1)}, bf16[256,128]{1,0:T(8,128)(2,1)}, u32[]{:S(2)}) %copy-start.1) | copy-done | bytes 65560
  4.7 0.0 copy-start.2
  4.7 0.8 %copy-done.2 = bf16[256,128]{1,0:T(8,128)(2,1)S(1)} copy-done((bf16[256,128]{1,0:T(8,128)(2,1)S(1)}, bf16[256,128]{1,0:T(8,128)(2,1)}, u32[]{:S(2)}) %copy-start.2) | copy-done | bytes 65560
  5.5 0.0 copy-start.3
  5.5 0.8 %copy-done.3 = f32[256,32]{0,1:T(8,128)S(1)} copy-done((f32[256,32]{0,1:T(8,128)S(1)}, f32[256,32]{0,1:T(8,128)}, u32[]{:S(2)}) %copy-start.3) | copy-done | bytes 32792
  6.3 0.0 copy-start.5
  6.3 0.7 %copy-done.5 = f32[4,1,32]{2,1,0:T(1,128)S(1)} copy-done((f32[4,1,32]{2,1,0:T(1,128)S(1)}, f32[4,1,32]{2,1,0:T(1,128)}, u32[]{:S(2)}) %copy-start.5) | copy-done | bytes 536
  7.0 0.0 copy-start.7
  7.0 0.7 %copy-done.7 = bf16[4,1,128]{2,0,1:T(4,128)(2,1)S(1)} copy-done((bf16[4,1,128]{2,0,1:T(4,128)(2,1)S(1)}, bf16[4,1,128]{2,0,1:T(4,128)(2,1)}, u32[]{:S(2)}) %copy-start.7) | copy-done | bytes 1048
  7.7 0.0 copy-start.8
  7.7 0.7 %copy-done.8 = f32[4,1]{0,1:T(1,128)S(1)} copy-done((f32[4,1]{0,1:T(1,128)S(1)}, f32[4,1]{0,1:T(1,128)}, u32[]{:S(2)}) %copy-start.8) | copy-done | bytes 40
  8.3 0.0 copy-start.9
  8.3 0.7 %copy-done.9 = s32[4,1]{0,1:T(1,128)S(1)} copy-done((s32[4,1]{0,1:T(1,128)S(1)}, s32[4,1]{0,1:T(1,128)}, u32[]{:S(2)}) %copy-start.9) | copy-done | bytes 40
  9.0 0.0 copy-start.10
  9.0 0.7 %copy-done.10 = s32[4,1]{0,1:T(1,128)S(1)} copy-done((s32[4,1]{0,1:T(1,128)S(1)}, s32[4,1]{0,1:T(1,128)}, u32[]{:S(2)}) %copy-start.10) | copy-done | bytes 40
  9.6 44.9 %shard_map.156 = (bf16[256,2048]{1,0:T(8,128)(2,1)S(1)}, bf16[1,4,2048]{2,1,0:T(4,128)(2,1)S(1)}, f32[1,4]{1,0:T(1,128)S(1)}, f32[1,2048,128]{2,1,0:T(8,128)S(1)}) custom-call(bf16[256,2048]{1,0:T(8,128)(2,1)S(1)} %copy-done, bf16[256,128]{1,0:T(8,128)(2,1)S(1)} %copy-done.1, bf16[256,128]{1,0:T(8,128)(2,1)S(1)} %copy-done.2, f32[32,256]{1,0:T(8,128)S(1)} %bitcast.9, ...), custom_call_target="tpu_custom_call" | custom-call | tf_op jit(solution)/shard_map/pallas_call | solution.py:481
  54.5 1.0 %copy.23 = bf16[256,2048]{1,0:T(8,128)(2,1)} copy(bf16[256,2048]{1,0:T(8,128)(2,1)S(1)} %get-tuple-element.16) | data formatting | bytes 2097152
  55.5 0.6 %copy.24 = bf16[4,1,2048]{2,0,1:T(4,128)(2,1)} copy(bf16[4,1,2048]{2,0,1:T(4,128)(2,1)S(1)} %bitcast.11) | data formatting | bytes 32768
  56.1 0.5 copy.25
  56.6 1.0 %copy.26 = f32[1,2048,128]{2,1,0:T(8,128)} copy(f32[1,2048,128]{2,1,0:T(8,128)S(1)} %get-tuple-element.19) | data formatting | bytes 2097152
Async XLA Ops:
  0.6 1.3 %copy-start.4 = (bf16[4,1,2048]{2,0,1:T(4,128)(2,1)S(1)}, bf16[4,1,2048]{2,0,1:T(4,128)(2,1)}, u32[]{:S(2)}) copy-start(bf16[4,1,2048]{2,0,1:T(4,128)(2,1)} %param.17) | copy-start | bytes 49156
  1.9 0.7 %copy-start.6 = (bf16[4,1,128]{2,0,1:T(4,128)(2,1)S(1)}, bf16[4,1,128]{2,0,1:T(4,128)(2,1)}, u32[]{:S(2)}) copy-start(bf16[4,1,128]{2,0,1:T(4,128)(2,1)} %param.18) | copy-start | bytes 3076
  2.6 1.2 %copy-start = (bf16[256,2048]{1,0:T(8,128)(2,1)S(1)}, bf16[256,2048]{1,0:T(8,128)(2,1)}, u32[]{:S(2)}) copy-start(bf16[256,2048]{1,0:T(8,128)(2,1)} %x_ref.1) | copy-start | bytes 3145732
  3.9 0.8 %copy-start.1 = (bf16[256,128]{1,0:T(8,128)(2,1)S(1)}, bf16[256,128]{1,0:T(8,128)(2,1)}, u32[]{:S(2)}) copy-start(bf16[256,128]{1,0:T(8,128)(2,1)} %keys_ref.1) | copy-start | bytes 196612
  4.7 0.8 %copy-start.2 = (bf16[256,128]{1,0:T(8,128)(2,1)S(1)}, bf16[256,128]{1,0:T(8,128)(2,1)}, u32[]{:S(2)}) copy-start(bf16[256,128]{1,0:T(8,128)(2,1)} %queries_ref.1) | copy-start | bytes 196612
  5.5 0.8 %copy-start.3 = (f32[256,32]{0,1:T(8,128)S(1)}, f32[256,32]{0,1:T(8,128)}, u32[]{:S(2)}) copy-start(f32[256,32]{0,1:T(8,128)} %param.16) | copy-start | bytes 98308
  6.3 0.7 %copy-start.5 = (f32[4,1,32]{2,1,0:T(1,128)S(1)}, f32[4,1,32]{2,1,0:T(1,128)}, u32[]{:S(2)}) copy-start(f32[4,1,32]{2,1,0:T(1,128)} %sd_ref.1) | copy-start | bytes 1540
  7.0 0.7 %copy-start.7 = (bf16[4,1,128]{2,0,1:T(4,128)(2,1)S(1)}, bf16[4,1,128]{2,0,1:T(4,128)(2,1)}, u32[]{:S(2)}) copy-start(bf16[4,1,128]{2,0,1:T(4,128)(2,1)} %param.19) | copy-start | bytes 3076
  7.7 0.7 %copy-start.8 = (f32[4,1]{0,1:T(1,128)S(1)}, f32[4,1]{0,1:T(1,128)}, u32[]{:S(2)}) copy-start(f32[4,1]{0,1:T(1,128)} %param.21) | copy-start | bytes 52
  8.3 0.7 %copy-start.9 = (s32[4,1]{0,1:T(1,128)S(1)}, s32[4,1]{0,1:T(1,128)}, u32[]{:S(2)}) copy-start(s32[4,1]{0,1:T(1,128)} %param.22) | copy-start | bytes 52
  9.0 0.7 %copy-start.10 = (s32[4,1]{0,1:T(1,128)S(1)}, s32[4,1]{0,1:T(1,128)}, u32[]{:S(2)}) copy-start(s32[4,1]{0,1:T(1,128)} %param.23) | copy-start | bytes 52

commit v3 on v2

--- a/solution.py
+++ b/solution.py
@@ -13,8 +13,10 @@
 PAIR = LANES // P_SIZE
 ROWS = 8
 HOP = 2
-SHARE = 2
-START = 2
+RELAY = 2
+SHARE = 4
+START = 4
+CORES = 2
 LOG2E = math.log2(math.e)
 MESH = pl.DeviceIdType.MESH
 F32 = jnp.float32
@@ -39,6 +41,23 @@
 def kernel(
     ns,
     nb,
+    x_in,
+    keys_in,
+    queries_in,
+    decay_in,
+    sv_in,
+    sk_in,
+    sq_in,
+    sd_in,
+    lp_in,
+    par_in,
+    fin_in,
+    len_in,
+    score_in,
+    out_ref,
+    so_ref,
+    rank_ref,
+    beam_ref,
     x_ref,
     keys_ref,
     queries_ref,
@@ -52,10 +71,7 @@
     fin_ref,
     len_ref,
     score_ref,
-    out_ref,
-    so_ref,
-    rank_ref,
-    beam_ref,
+    in_sem,
     sums_ref,
     cols,
     grown,
@@ -98,6 +114,29 @@
     dchunks = dwidth // LANES
     last = ns - 1
 
+    loads = [
+        pltpu.make_async_copy(source, here, in_sem.at[i])
+        for i, (source, here) in enumerate(
+            (
+                (decay_in, decay_ref),
+                (keys_in, keys_ref),
+                (x_in, x_ref),
+                (fin_in, fin_ref),
+                (sd_in, sd_ref),
+                (sv_in, sv_ref),
+                (sk_in, sk_ref),
+                (lp_in, lp_ref),
+                (par_in, par_ref),
+                (queries_in, queries_ref),
+                (sq_in, sq_ref),
+                (len_in, len_ref),
+                (score_in, score_ref),
+            )
+        )
+    ]
+    for load in loads:
+        load.start()
+
     barrier = pltpu.get_barrier_semaphore()
 
     def peer(i):
@@ -134,13 +173,22 @@
             device_id_type=MESH,
         )
 
+    owner = (s * dchunks) // chunks
+    mates = nb // CORES
+    chip, core = b // CORES, lax.rem(b, CORES)
+    other_core = chip * CORES + (CORES - 1 - core)
+    is_owner = b == owner
+    relays = (core == lax.rem(owner, CORES)) & (b != owner)
+    near = relays | (chip == owner // CORES)
+
     def f_copy(kk, i):
+        to = other_core if i == 0 else lax.rem(chip + i, mates) * CORES + core
         return pltpu.make_async_remote_copy(
             src_ref=final.at[kk],
             dst_ref=final.at[kk],
-            send_sem=f_ss.at[kk, i - 1],
+            send_sem=f_ss.at[kk, i],
             recv_sem=f_rs.at[kk],
-            device_id=(g, s, peer(i)),
+            device_id=(g, s, to),
             device_id_type=MESH,
         )
 
@@ -170,6 +218,9 @@
     def place(k):
         return lax.rem(b * chunks + k, dchunks)
 
+    for load in loads[:3]:
+        load.wait()
+
     row_id = lax.broadcasted_iota(jnp.int32, (toks, toks), 0)
     col_id = lax.broadcasted_iota(jnp.int32, (toks, toks), 1)
     upper = (row_id <= col_id).astype(F32).astype(BF16)
@@ -196,6 +247,36 @@
         grown[k] = jnp.exp2(column)
         own[k, n : n + ROWS, :] = jnp.broadcast_to(jnp.exp2(end), (ROWS, LANES))
         return carry
+
+    make_state(0, 0)
+
+    met = nb - 1 + jnp.where(s > 0, 1, 0) + jnp.where(s < last, 1, 0)
+    pl.semaphore_wait(barrier, met)
+
+    def first_sends(k):
+        @pl.when((s == 0) & (s < last))
+        def _():
+            up_copy(own.at[k, pl.ds(0, n)], k).start()
+
+        @pl.when((s == last) & (s > target(k)))
+        def _():
+            dn_copy(own.at[k], k).start()
+
+    first_sends(0)
+
+    def state_and_send(k, carry):
+        make_state(k, 0)
+        first_sends(k)
+        return carry
+
+    at_edge = (s == 0) | (s == last)
+
+    @pl.when(at_edge)
+    def _():
+        lax.fori_loop(1, chunks, state_and_send, 0)
+
+    for load in loads[3:]:
+        load.wait()
 
     def column_of(row):
         row = row.astype(F32)
@@ -225,32 +306,9 @@
     small[b, 4 * steps : 4 * steps + 1, :] = jnp.full((1, LANES), score_ref[0], F32)
     small[b, 4 * steps + 1 : 4 * steps + 2, :] = jnp.full((1, LANES), len_ref[0], jnp.int32).astype(F32)
 
-    make_state(0, 0)
-
-    met = nb - 1 + jnp.where(s > 0, 1, 0) + jnp.where(s < last, 1, 0)
-    pl.semaphore_wait(barrier, met)
-
     for i in range(1, nb):
         m_copy(i).start()
         v_copy(i).start()
-
-    def first_sends(k):
-        @pl.when((s == 0) & (s < last))
-        def _():
-            up_copy(own.at[k, pl.ds(0, n)], k).start()
-
-        @pl.when((s == last) & (s > target(k)))
-        def _():
-            dn_copy(own.at[k], k).start()
-
-    first_sends(0)
-
-    def state_and_send(k, carry):
-        make_state(k, 0)
-        first_sends(k)
-        return carry
-
-    lax.fori_loop(1, chunks, state_and_send, 0)
 
     scores[...] = jnp.where(row_id >= col_id, mm(queries_ref[...], keys_t[...]), 0.0)
 
@@ -332,17 +390,21 @@
         beam_ref[0, rows, :] = (state * dec_d[steps - 1 : steps, at]).T + outer
 
     def await_and_finish(kk):
-        @pl.when(b != (s * dchunks) // chunks)
-        def _():
-            f_copy(kk, 1).wait_recv()
+        @pl.when(b != owner)
+        def _():
+            f_copy(kk, 0).wait_recv()
+
+        @pl.when(relays)
+        def _():
+            f_copy(kk, 0).start()
 
         finish(kk)
 
     up_lag = s * HOP
     dn_lag = (last - s) * HOP
-    own_lag = jnp.maximum(jnp.maximum(up_lag, dn_lag), START + steps - SHARE)
+    own_lag = jnp.maximum(jnp.maximum(up_lag, dn_lag), START + steps)
     first = lax.rem(s * dchunks, chunks)
-    slots = chunks + max(last * HOP, START + steps - SHARE) + SHARE
+    slots = chunks + max(last * HOP, START + steps) + SHARE
 
     def inside(k):
         return (k >= 0) & (k < chunks)
@@ -395,7 +457,7 @@
         def _():
             final[kk] = up_out[k]
 
-        for i in range(1, nb):
+        for i in range(mates):
             f_copy(kk, i).start()
 
     def body(slot, carry):
@@ -409,6 +471,10 @@
                         v_copy(i).wait_recv()
                 prepare(step)
 
+        @pl.when((slot > 0) & (slot < chunks) & (s > 0) & (s < last))
+        def _():
+            make_state(slot, 0)
+
         @pl.when(slot < chunks)
         def _():
             make_inner(slot)
@@ -429,7 +495,7 @@
         def _():
             share_final(at_end)
 
-        kk = slot - own_lag - SHARE - first
+        kk = slot - own_lag - first - jnp.where(is_owner, 0, jnp.where(near, RELAY, SHARE))
 
         @pl.when((kk >= 0) & (kk < dchunks))
         def _():
@@ -457,12 +523,20 @@
 
         @pl.when(s == target(k))
         def _():
-            for i in range(1, nb):
+            for i in range(mates):
                 f_copy(place(k), i).wait_send()
 
         return carry
 
     lax.fori_loop(0, chunks, drain, 0)
+
+    @pl.when(relays)
+    def _():
+        def drain_relay(kk, carry):
+            f_copy(kk, 0).wait_send()
+            return carry
+
+        lax.fori_loop(0, dchunks, drain_relay, 0)
 
 
 def on_device(ns, nb, *args):
@@ -475,9 +549,10 @@
     small_rows = -(-(4 * steps + 2) // ROWS) * ROWS
     dma = pltpu.SemaphoreType.DMA
     spec = pl.BlockSpec(memory_space=pltpu.VMEM)
-    scalar = pl.BlockSpec(memory_space=pltpu.SMEM)
+    outside = pl.BlockSpec(memory_space=pl.ANY)
     peers = max(nb - 1, 1)
     turn = lambda a: jnp.transpose(a, (1, 0, 2))
+    inputs = (x, keys, queries, decay.T, turn(sv), turn(sk), turn(sq), sd, lp.T, par.T, fin.T, lens, score)
     prompt, step_out, ranked, states = pl.pallas_call(
         functools.partial(kernel, ns, nb),
         out_shape=(
@@ -486,9 +561,12 @@
             jax.ShapeDtypeStruct((1, steps), F32),
             jax.ShapeDtypeStruct((1, dwidth, n), F32),
         ),
-        in_specs=[spec] * 11 + [scalar] * 2,
+        in_specs=[outside] * 13,
         out_specs=(spec,) * 4,
         scratch_shapes=[
+            *[pltpu.VMEM(a.shape, a.dtype) for a in inputs[:11]],
+            *[pltpu.SMEM(a.shape, a.dtype) for a in inputs[11:]],
+            dma((len(inputs),)),
             pltpu.VMEM((heads, toks), F32),
             pltpu.VMEM((heads, toks, LANES), F32),
             pltpu.VMEM((chunks, toks, LANES), F32),
@@ -513,7 +591,7 @@
             dma((chunks,)),
             dma((chunks,)),
             dma((chunks,)),
-            dma((dchunks, peers)),
+            dma((dchunks, nb // CORES)),
             dma((dchunks,)),
             dma((peers,)),
             dma((peers,)),
@@ -521,9 +599,9 @@
             dma((peers,)),
         ],
         compiler_params=pltpu.CompilerParams(
-            collective_id=0, has_side_effects=True, vmem_limit_bytes=40 * 1024 * 1024
+            collective_id=0, has_side_effects=True, vmem_limit_bytes=60 * 1024 * 1024
         ),
-    )(x, keys, queries, decay.T, turn(sv), turn(sk), turn(sq), sd, lp.T, par.T, fin.T, lens, score)
+    )(*inputs)
     return prompt, turn(step_out), ranked.T, states
 
 

time: 58 us -> 52.4 us (0.903)
  local copies, waits for them, and re-layouts: 10.7 us -> 4.49 us
  Pallas kernels: 44.9 us -> 45.8 us
    unnamed x26 -> x10, local copies, waits for them, and re-layouts: 10.7 us -> 4.49 us
    pallas_call x1, Pallas kernels: 44.9 us -> 45.8 us  [on_device(): pl.pallas_call(functools.partial(kernel, ns, nb), out_shape=(jax.ShapeDty...]
where the time goes in v3:
time: 52.4 us; the launch traced here: 52.2 us
  Pallas kernels  45.8 us (87%)
  local copies, waits for them, and re-layouts  4.49 us (9%)
  between operations  1.95 us (4%)
    pallas_call x1, Pallas kernels, on_device(): pl.pallas_call(functools.partial(kernel, ns, nb), out_shape=(jax.ShapeDty...  45.8 us
    unnamed x10, local copies, waits for them, and re-layouts  4.49 us

profile of v3, /device:TPU:3, one launch (start us, length us, event | category | flops | bytes accessed | tf_op | source)
XLA Modules:
  0.0 52.2 jit_solution(16321865945786222599)
XLA Ops:
  1.9 45.8 %shard_map.156 = (bf16[256,2048]{1,0:T(8,128)(2,1)}, bf16[1,4,2048]{2,1,0:T(4,128)(2,1)}, f32[1,4]{1,0:T(1,128)}, f32[1,2048,128]{2,1,0:T(8,128)}) custom-call(bf16[256,2048]{1,0:T(8,128)(2,1)} %x_in.1, bf16[256,128]{1,0:T(8,128)(2,1)} %keys_in.1, bf16[256,128]{1,0:T(8,128)(2,1)} %queries_in.1, f32[32,256]{1,0:T(8,128)} %bitcast.9, ...), custom_call_target="tpu_custom_call" | custom-call | tf_op jit(solution)/shard_map/pallas_call | solution.py:556
  47.7 0.0 copy-start.1
  47.7 0.0 copy-start
  47.7 2.4 %copy.23 = bf16[256,2048]{1,0:T(8,128)(2,1)} copy(bf16[256,2048]{1,0:T(8,128)(2,1)} %get-tuple-element.16) | data formatting | bytes 2097152
  50.1 0.0 copy-done.1
  50.1 0.0 copy-start.2
  50.1 0.6 %copy.24 = bf16[4,1,2048]{2,0,1:T(4,128)(2,1)} copy(bf16[4,1,2048]{2,0,1:T(4,128)(2,1)S(1)} %bitcast.11) | data formatting | bytes 32768
  50.8 0.0 copy-done.2
  50.8 0.5 copy.25
  51.3 0.0 copy-done
  51.3 1.0 %copy.26 = f32[1,2048,128]{2,1,0:T(8,128)} copy(f32[1,2048,128]{2,1,0:T(8,128)S(1)} %copy-done) | data formatting | bytes 2097152
Async XLA Ops:
  47.7 2.4 %copy-start.1 = (bf16[1,4,2048]{2,1,0:T(4,128)(2,1)S(1)}, bf16[1,4,2048]{2,1,0:T(4,128)(2,1)}, u32[]{:S(2)}) copy-start(bf16[1,4,2048]{2,1,0:T(4,128)(2,1)} %get-tuple-element.9) | copy-start | bytes 49156
  47.7 3.5 %copy-start = (f32[1,2048,128]{2,1,0:T(8,128)S(1)}, f32[1,2048,128]{2,1,0:T(8,128)}, u32[]{:S(2)}) copy-start(f32[1,2048,128]{2,1,0:T(8,128)} %get-tuple-element.19) | copy-start | bytes 3145732
  50.1 0.6 %copy-start.2 = (f32[1,4]{1,0:T(1,128)S(1)}, f32[1,4]{1,0:T(1,128)}, u32[]{:S(2)}) copy-start(f32[1,4]{1,0:T(1,128)} %get-tuple-element.10) | copy-start | bytes 52

commit v4 on v3

--- a/solution.py
+++ b/solution.py
@@ -12,9 +12,9 @@
 LANES = 128
 PAIR = LANES // P_SIZE
 ROWS = 8
-HOP = 2
-RELAY = 2
-SHARE = 4
+HOP = 3
+RELAY = 3
+SHARE = 6
 START = 4
 CORES = 2
 LOG2E = math.log2(math.e)
@@ -102,6 +102,9 @@
     v_rs,
     m_ss,
     m_rs,
+    beam_out,
+    out_sem,
+    beam_sem,
 ):
     g = lax.axis_index("groups")
     s = lax.axis_index("seq")
@@ -153,6 +156,9 @@
     for i in range(1, nb):
         pl.semaphore_signal(barrier, inc=1, device_id=(g, s, peer(i)), device_id_type=MESH)
 
+    def lanes_of(k):
+        return pl.ds(pl.multiple_of(k * LANES, LANES), LANES)
+
     def up_copy(src, k):
         return pltpu.make_async_remote_copy(
             src_ref=src,
@@ -212,6 +218,13 @@
             device_id_type=MESH,
         )
 
+    def out_copy(k):
+        return pltpu.make_async_copy(inner_ref.at[k], out_ref.at[:, lanes_of(k)], out_sem.at[k])
+
+    def beam_copy(kk):
+        rows = pl.ds(pl.multiple_of(kk * LANES, LANES), LANES)
+        return pltpu.make_async_copy(beam_out.at[kk], beam_ref.at[0, rows], beam_sem.at[kk])
+
     def target(k):
         return (b * chunks + k) // dchunks
 
@@ -235,9 +248,6 @@
         column = jnp.broadcast_to(row, (LANES, toks)).T
         cols[head] = column
         return column
-
-    def lanes_of(k):
-        return pl.ds(pl.multiple_of(k * LANES, LANES), LANES)
 
     def make_state(k, carry):
         column = jnp.where(left, make_column(k * PAIR), make_column(k * PAIR + 1))
@@ -386,8 +396,8 @@
         keep = pad[:, 0:1]
         dec_add[:, at] = keep * (dec_d[:, at] * read) + dec_add[:, at]
         outer = mm_first(dec_cv[:, at].astype(BF16), dec_k[...].astype(BF16))
-        rows = pl.ds(pl.multiple_of(kk * LANES, LANES), LANES)
-        beam_ref[0, rows, :] = (state * dec_d[steps - 1 : steps, at]).T + outer
+        beam_out[kk] = (state * dec_d[steps - 1 : steps, at]).T + outer
+        beam_copy(kk).start()
 
     def await_and_finish(kk):
         @pl.when(b != owner)
@@ -431,7 +441,7 @@
         @pl.when(s == 0)
         def _():
             up_out[k] = own[k, 0:n, :]
-            out_ref[:, lanes_of(k)] = inner_ref[k].astype(BF16)
+            out_copy(k).start()
 
         @pl.when(s > 0)
         def _():
@@ -443,7 +453,8 @@
                 up_copy(up_out.at[k], k).start()
 
             carried = mm(queries_ref[...], up_recv[k].astype(BF16)) * grown[k]
-            out_ref[:, lanes_of(k)] = (inner_ref[k] + carried).astype(BF16)
+            inner_ref[k] = inner_ref[k] + carried
+            out_copy(k).start()
 
     def share_final(k):
         kk = place(k)
@@ -479,13 +490,18 @@
         def _():
             make_inner(slot)
 
+        down = slot - dn_lag
+        goes_down = inside(down) & (s > target(down)) & (s < last)
+
+        @pl.when(goes_down & (2 * s >= ns))
+        def _():
+            forward_down(down)
+
         @pl.when(inside(slot - up_lag))
         def _():
             take_up(slot - up_lag)
 
-        down = slot - dn_lag
-
-        @pl.when(inside(down) & (s > target(down)) & (s < last))
+        @pl.when(goes_down & (2 * s < ns))
         def _():
             forward_down(down)
 
@@ -529,6 +545,18 @@
         return carry
 
     lax.fori_loop(0, chunks, drain, 0)
+
+    def drain_results(k, carry):
+        out_copy(k).wait()
+        return carry
+
+    lax.fori_loop(0, chunks, drain_results, 0)
+
+    def drain_states(kk, carry):
+        beam_copy(kk).wait()
+        return carry
+
+    lax.fori_loop(0, dchunks, drain_states, 0)
 
     @pl.when(relays)
     def _():
@@ -556,13 +584,13 @@
     prompt, step_out, ranked, states = pl.pallas_call(
         functools.partial(kernel, ns, nb),
         out_shape=(
-            jax.ShapeDtypeStruct((toks, width), BF16),
+            jax.ShapeDtypeStruct((toks, width), F32),
             jax.ShapeDtypeStruct((1, steps, dwidth), BF16),
             jax.ShapeDtypeStruct((1, steps), F32),
             jax.ShapeDtypeStruct((1, dwidth, n), F32),
         ),
         in_specs=[outside] * 13,
-        out_specs=(spec,) * 4,
+        out_specs=(outside, spec, spec, outside),
         scratch_shapes=[
             *[pltpu.VMEM(a.shape, a.dtype) for a in inputs[:11]],
             *[pltpu.SMEM(a.shape, a.dtype) for a in inputs[11:]],
@@ -597,12 +625,15 @@
             dma((peers,)),
             dma((peers,)),
             dma((peers,)),
+            pltpu.VMEM((dchunks, LANES, n), F32),
+            dma((chunks,)),
+            dma((dchunks,)),
         ],
         compiler_params=pltpu.CompilerParams(
             collective_id=0, has_side_effects=True, vmem_limit_bytes=60 * 1024 * 1024
         ),
     )(*inputs)
-    return prompt, turn(step_out), ranked.T, states
+    return prompt.astype(BF16), turn(step_out), ranked.T, states
 
 
 def solution(mesh):

time: 52.4 us -> 51.3 us (0.979)
  other arithmetic: 0 us -> 2.8 us
  local copies, waits for them, and re-layouts: 4.49 us -> 2.1 us
  Pallas kernels: 45.8 us -> 44.3 us
    convert_element_type x0 -> x1, other arithmetic: none -> 2.8 us  [on_device(): return (prompt.astype(BF16), turn(step_out), ranked.T, states)]
    unnamed x10 -> x9, local copies, waits for them, and re-layouts: 4.49 us -> 2.1 us
    pallas_call x1, Pallas kernels: 45.8 us -> 44.3 us  [on_device(): pl.pallas_call(functools.partial(kernel, ns, nb), out_shape=(jax.ShapeDty...]
where the time goes in v4:
time: 51.3 us; the launch traced here: 51.1 us
  Pallas kernels  44.3 us (86%)
  other arithmetic  2.8 us (5%)
  local copies, waits for them, and re-layouts  2.1 us (4%)
  between operations  1.96 us (4%)
    pallas_call x1, Pallas kernels, on_device(): pl.pallas_call(functools.partial(kernel, ns, nb), out_shape=(jax.ShapeDty...  44.3 us
    convert_element_type x1, other arithmetic, on_device(): return (prompt.astype(BF16), turn(step_out), ranked.T, states)  2.8 us
    unnamed x9, local copies, waits for them, and re-layouts  2.1 us

profile of v4, /device:TPU:3, one launch (start us, length us, event | category | flops | bytes accessed | tf_op | source)
XLA Modules:
  0.0 51.1 jit_solution(15404649749547592143)
XLA Ops:
  1.9 44.3 %shard_map.156 = (f32[256,2048]{1,0:T(8,128)}, bf16[1,4,2048]{2,1,0:T(4,128)(2,1)}, f32[1,4]{1,0:T(1,128)}, f32[1,2048,128]{2,1,0:T(8,128)}) custom-call(bf16[256,2048]{1,0:T(8,128)(2,1)} %x_in.1, bf16[256,128]{1,0:T(8,128)(2,1)} %keys_in.1, bf16[256,128]{1,0:T(8,128)(2,1)} %queries_in.1, f32[32,256]{1,0:T(8,128)} %bitcast.9, bf16[1,4,2048]{2,1,0:T(4,128)(2,1)} %bitcast.10, ...), custom_call_target="tpu_custom_call" | custom-call | tf_op jit(solution)/shard_map/pallas_call | solution.py:584
  46.2 0.0 copy-start.1
  46.2 0.0 copy-start.2
  46.2 0.0 copy-start
  46.2 2.8 %convert_element_type.3 = bf16[256,2048]{1,0:T(8,128)(2,1)} convert(f32[256,2048]{1,0:T(8,128)} %get-tuple-element.8) | non-fusion elementwise | flops 524288 | bytes 3145728 | tf_op jit(solution)/shard_map/convert_element_type | solution.py:636
  49.0 0.0 copy-done.1
  49.0 0.6 %copy.22 = bf16[4,1,2048]{2,0,1:T(4,128)(2,1)} copy(bf16[4,1,2048]{2,0,1:T(4,128)(2,1)S(1)} %bitcast.11) | data formatting | bytes 32768
  49.7 0.0 copy-done.2
  49.7 0.5 copy.23
  50.2 0.0 copy-done
  50.2 1.0 %copy.24 = f32[1,2048,128]{2,1,0:T(8,128)} copy(f32[1,2048,128]{2,1,0:T(8,128)S(1)} %copy-done) | data formatting | bytes 2097152
Async XLA Ops:
  46.2 2.8 %copy-start.1 = (bf16[1,4,2048]{2,1,0:T(4,128)(2,1)S(1)}, bf16[1,4,2048]{2,1,0:T(4,128)(2,1)}, u32[]{:S(2)}) copy-start(bf16[1,4,2048]{2,1,0:T(4,128)(2,1)} %get-tuple-element.9) | copy-start | bytes 49156
  46.2 3.4 %copy-start.2 = (f32[1,4]{1,0:T(1,128)S(1)}, f32[1,4]{1,0:T(1,128)}, u32[]{:S(2)}) copy-start(f32[1,4]{1,0:T(1,128)} %get-tuple-element.10) | copy-start | bytes 52
  46.2 3.9 %copy-start = (f32[1,2048,128]{2,1,0:T(8,128)S(1)}, f32[1,2048,128]{2,1,0:T(8,128)}, u32[]{:S(2)}) copy-start(f32[1,2048,128]{2,1,0:T(8,128)} %get-tuple-element.19) | copy-start | bytes 3145732

commit v5 on v3

--- a/solution.py
+++ b/solution.py
@@ -12,11 +12,12 @@
 LANES = 128
 PAIR = LANES // P_SIZE
 ROWS = 8
-HOP = 2
-RELAY = 2
-SHARE = 4
+HOP = 3
+RELAY = 3
+SHARE = 6
 START = 4
 CORES = 2
+PIECES = 2
 LOG2E = math.log2(math.e)
 MESH = pl.DeviceIdType.MESH
 F32 = jnp.float32
@@ -153,22 +154,36 @@
     for i in range(1, nb):
         pl.semaphore_signal(barrier, inc=1, device_id=(g, s, peer(i)), device_id_type=MESH)
 
-    def up_copy(src, k):
+    def lanes_of(k):
+        return pl.ds(pl.multiple_of(k * LANES, LANES), LANES)
+
+    piece = n // PIECES
+
+    def up_rows(p, top=0):
+        return pl.ds(top + p * piece, piece)
+
+    def dn_rows(p):
+        return pl.ds(0, ROWS + piece) if p == 0 else up_rows(p, ROWS)
+
+    def up_copy(src, k, p):
         return pltpu.make_async_remote_copy(
             src_ref=src,
-            dst_ref=up_recv.at[k],
-            send_sem=up_ss.at[k],
-            recv_sem=up_rs.at[k],
+            dst_ref=up_recv.at[k, up_rows(p)],
+            send_sem=up_ss.at[k, p],
+            recv_sem=up_rs.at[k, p],
             device_id=(g, lax.rem(s + 1, ns), b),
             device_id_type=MESH,
         )
 
-    def dn_copy(src, k):
+    def up_sent(k, p):
+        return up_copy(up_out.at[k, up_rows(p)], k, p)
+
+    def dn_copy(src, k, p):
         return pltpu.make_async_remote_copy(
-            src_ref=src,
-            dst_ref=dn_recv.at[k],
-            send_sem=dn_ss.at[k],
-            recv_sem=dn_rs.at[k],
+            src_ref=src.at[k, dn_rows(p)],
+            dst_ref=dn_recv.at[k, dn_rows(p)],
+            send_sem=dn_ss.at[k, p],
+            recv_sem=dn_rs.at[k, p],
             device_id=(g, lax.rem(s + ns - 1, ns), b),
             device_id_type=MESH,
         )
@@ -236,16 +251,13 @@
         cols[head] = column
         return column
 
-    def lanes_of(k):
-        return pl.ds(pl.multiple_of(k * LANES, LANES), LANES)
-
     def make_state(k, carry):
         column = jnp.where(left, make_column(k * PAIR), make_column(k * PAIR + 1))
         end = column[toks - 1 : toks, :]
         scaled = (x_ref[:, lanes_of(k)].astype(F32) * jnp.exp2(end - column)).astype(BF16)
-        own[k, 0:n, :] = mm(keys_t[...], scaled)
+        own[k, ROWS : ROWS + n, :] = mm(keys_t[...], scaled)
         grown[k] = jnp.exp2(column)
-        own[k, n : n + ROWS, :] = jnp.broadcast_to(jnp.exp2(end), (ROWS, LANES))
+        own[k, 0:ROWS, :] = jnp.broadcast_to(jnp.exp2(end), (ROWS, LANES))
         return carry
 
     make_state(0, 0)
@@ -256,11 +268,13 @@
     def first_sends(k):
         @pl.when((s == 0) & (s < last))
         def _():
-            up_copy(own.at[k, pl.ds(0, n)], k).start()
+            for p in range(PIECES):
+                up_copy(own.at[k, up_rows(p, ROWS)], k, p).start()
 
         @pl.when((s == last) & (s > target(k)))
         def _():
-            dn_copy(own.at[k], k).start()
+            for p in range(PIECES):
+                dn_copy(own, k, p).start()
 
     first_sends(0)
 
@@ -373,11 +387,14 @@
             rank_ref[:, step : step + 1] = (mine - best)[:, 0:1]
 
     def forward_down(k):
-        dn_copy(dn_out.at[k], k).wait_recv()
-        shrink = dn_recv[k, n : n + 1, :]
-        dn_out[k, 0:n, :] = dn_recv[k, 0:n, :] + shrink * own[k, 0:n, :]
-        dn_out[k, n : n + ROWS, :] = dn_recv[k, n : n + ROWS, :] * own[k, n : n + ROWS, :]
-        dn_copy(dn_out.at[k], k).start()
+        for p in range(PIECES):
+            dn_copy(dn_out, k, p).wait_recv()
+            shrink = dn_recv[k, 0:1, :]
+            rows = up_rows(p, ROWS)
+            if p == 0:
+                dn_out[k, 0:ROWS, :] = dn_recv[k, 0:ROWS, :] * own[k, 0:ROWS, :]
+            dn_out[k, rows, :] = dn_recv[k, rows, :] + shrink * own[k, rows, :]
+            dn_copy(dn_out, k, p).start()
 
     def finish(kk):
         at = lanes_of(kk)
@@ -430,17 +447,20 @@
     def take_up(k):
         @pl.when(s == 0)
         def _():
-            up_out[k] = own[k, 0:n, :]
+            up_out[k] = own[k, ROWS : ROWS + n, :]
             out_ref[:, lanes_of(k)] = inner_ref[k].astype(BF16)
 
         @pl.when(s > 0)
         def _():
-            up_copy(up_out.at[k], k).wait_recv()
-            up_out[k] = own[k, n : n + 1, :] * up_recv[k] + own[k, 0:n, :]
-
-            @pl.when(s < last)
-            def _():
-                up_copy(up_out.at[k], k).start()
+            for p in range(PIECES):
+                up_sent(k, p).wait_recv()
+                up_out[k, up_rows(p), :] = (
+                    own[k, 0:1, :] * up_recv[k, up_rows(p), :] + own[k, up_rows(p, ROWS), :]
+                )
+
+                @pl.when(s < last)
+                def _():
+                    up_sent(k, p).start()
 
             carried = mm(queries_ref[...], up_recv[k].astype(BF16)) * grown[k]
             out_ref[:, lanes_of(k)] = (inner_ref[k] + carried).astype(BF16)
@@ -450,8 +470,9 @@
 
         @pl.when(s < last)
         def _():
-            dn_copy(dn_out.at[k], k).wait_recv()
-            final[kk] = dn_recv[k, n : n + 1, :] * up_out[k] + dn_recv[k, 0:n, :]
+            for p in range(PIECES):
+                dn_copy(dn_out, k, p).wait_recv()
+            final[kk] = dn_recv[k, 0:1, :] * up_out[k] + dn_recv[k, ROWS : ROWS + n, :]
 
         @pl.when(s == last)
         def _():
@@ -479,13 +500,18 @@
         def _():
             make_inner(slot)
 
+        down = slot - dn_lag
+        goes_down = inside(down) & (s > target(down)) & (s < last)
+
+        @pl.when(goes_down & (2 * s >= ns))
+        def _():
+            forward_down(down)
+
         @pl.when(inside(slot - up_lag))
         def _():
             take_up(slot - up_lag)
 
-        down = slot - dn_lag
-
-        @pl.when(inside(down) & (s > target(down)) & (s < last))
+        @pl.when(goes_down & (2 * s < ns))
         def _():
             forward_down(down)
 
@@ -515,11 +541,13 @@
     def drain(k, carry):
         @pl.when(s < last)
         def _():
-            up_copy(up_out.at[k], k).wait_send()
+            for p in range(PIECES):
+                up_sent(k, p).wait_send()
 
         @pl.when(s > target(k))
         def _():
-            dn_copy(dn_out.at[k], k).wait_send()
+            for p in range(PIECES):
+                dn_copy(dn_out, k, p).wait_send()
 
         @pl.when(s == target(k))
         def _():
@@ -587,10 +615,10 @@
             pltpu.VMEM((2 * ROWS, dwidth), F32),
             pltpu.VMEM((2 * ROWS, n), F32),
             pltpu.VMEM((ROWS, n), F32),
-            dma((chunks,)),
-            dma((chunks,)),
-            dma((chunks,)),
-            dma((chunks,)),
+            dma((chunks, PIECES)),
+            dma((chunks, PIECES)),
+            dma((chunks, PIECES)),
+            dma((chunks, PIECES)),
             dma((dchunks, nb // CORES)),
             dma((dchunks,)),
             dma((peers,)),

time: 52.4 us -> 51.1 us (0.975)
  Pallas kernels: 45.8 us -> 44.5 us
    pallas_call x1, Pallas kernels: 45.8 us -> 44.5 us  [on_device(): pl.pallas_call(functools.partial(kernel, ns, nb), out_shape=(jax.ShapeDty...]
where the time goes in v5:
time: 51.1 us; the launch traced here: 51 us
  Pallas kernels  44.5 us (87%)
  local copies, waits for them, and re-layouts  4.49 us (9%)
  between operations  1.95 us (4%)
    pallas_call x1, Pallas kernels, on_device(): pl.pallas_call(functools.partial(kernel, ns, nb), out_shape=(jax.ShapeDty...  44.5 us
    unnamed x10, local copies, waits for them, and re-layouts  4.49 us

profile of v5, /device:TPU:3, one launch (start us, length us, event | category | flops | bytes accessed | tf_op | source)
XLA Modules:
  0.0 51.0 jit_solution(4263587778546787973)
XLA Ops:
  1.9 44.5 %shard_map.156 = (bf16[256,2048]{1,0:T(8,128)(2,1)}, bf16[1,4,2048]{2,1,0:T(4,128)(2,1)}, f32[1,4]{1,0:T(1,128)}, f32[1,2048,128]{2,1,0:T(8,128)}) custom-call(bf16[256,2048]{1,0:T(8,128)(2,1)} %x_in.1, bf16[256,128]{1,0:T(8,128)(2,1)} %keys_in.1, bf16[256,128]{1,0:T(8,128)(2,1)} %queries_in.1, f32[32,256]{1,0:T(8,128)} %bitcast.9, ...), custom_call_target="tpu_custom_call" | custom-call | tf_op jit(solution)/shard_map/pallas_call | solution.py:584
  46.4 0.0 copy-start.1
  46.5 0.0 copy-start
  46.5 2.4 %copy.23 = bf16[256,2048]{1,0:T(8,128)(2,1)} copy(bf16[256,2048]{1,0:T(8,128)(2,1)} %get-tuple-element.16) | data formatting | bytes 2097152
  48.9 0.0 copy-done.1
  48.9 0.0 copy-start.2
  48.9 0.6 %copy.24 = bf16[4,1,2048]{2,0,1:T(4,128)(2,1)} copy(bf16[4,1,2048]{2,0,1:T(4,128)(2,1)S(1)} %bitcast.11) | data formatting | bytes 32768
  49.5 0.0 copy-done.2
  49.5 0.5 %copy.25 = f32[4,1]{0,1:T(1,128)} copy(f32[4,1]{0,1:T(1,128)S(1)} %bitcast.17) | data formatting | bytes 32
  50.0 0.0 copy-done
  50.0 1.0 %copy.26 = f32[1,2048,128]{2,1,0:T(8,128)} copy(f32[1,2048,128]{2,1,0:T(8,128)S(1)} %copy-done) | data formatting | bytes 2097152
Async XLA Ops:
  46.4 2.4 %copy-start.1 = (bf16[1,4,2048]{2,1,0:T(4,128)(2,1)S(1)}, bf16[1,4,2048]{2,1,0:T(4,128)(2,1)}, u32[]{:S(2)}) copy-start(bf16[1,4,2048]{2,1,0:T(4,128)(2,1)} %get-tuple-element.9) | copy-start | bytes 49156
  46.5 3.5 %copy-start = (f32[1,2048,128]{2,1,0:T(8,128)S(1)}, f32[1,2048,128]{2,1,0:T(8,128)}, u32[]{:S(2)}) copy-start(f32[1,2048,128]{2,1,0:T(8,128)} %get-tuple-element.19) | copy-start | bytes 3145732
  48.9 0.6 %copy-start.2 = (f32[1,4]{1,0:T(1,128)S(1)}, f32[1,4]{1,0:T(1,128)}, u32[]{:S(2)}) copy-start(f32[1,4]{1,0:T(1,128)} %get-tuple-element.10) | copy-start | bytes 52

commit v6 on v5

--- a/solution.py
+++ b/solution.py
@@ -17,7 +17,7 @@
 SHARE = 6
 START = 4
 CORES = 2
-PIECES = 2
+PIECES = 1
 LOG2E = math.log2(math.e)
 MESH = pl.DeviceIdType.MESH
 F32 = jnp.float32
@@ -278,16 +278,23 @@
 
     first_sends(0)
 
-    def state_and_send(k, carry):
-        make_state(k, 0)
-        first_sends(k)
+    together = 2 if chunks % 2 == 0 else 1
+
+    def state_and_send(group, carry):
+        for i in range(together):
+            make_state(group * together + i, 0)
+        for i in range(together):
+            first_sends(group * together + i)
         return carry
 
     at_edge = (s == 0) | (s == last)
 
     @pl.when(at_edge)
     def _():
-        lax.fori_loop(1, chunks, state_and_send, 0)
+        for i in range(1, together):
+            make_state(i, 0)
+            first_sends(i)
+        lax.fori_loop(1, chunks // together, state_and_send, 0)
 
     for load in loads[3:]:
         load.wait()
@@ -492,13 +499,17 @@
                         v_copy(i).wait_recv()
                 prepare(step)
 
-        @pl.when((slot > 0) & (slot < chunks) & (s > 0) & (s < last))
-        def _():
-            make_state(slot, 0)
-
-        @pl.when(slot < chunks)
-        def _():
-            make_inner(slot)
+        starts = (slot < chunks) & (lax.rem(slot, together) == 0)
+
+        @pl.when(starts & (s > 0) & (s < last))
+        def _():
+            for i in range(together):
+                make_state(slot + i, 0)
+
+        @pl.when(starts)
+        def _():
+            for i in range(together):
+                make_inner(slot + i)
 
         down = slot - dn_lag
         goes_down = inside(down) & (s > target(down)) & (s < last)

time: 51.1 us -> 51.4 us (level)
  no operation moved by 1% of the time
where the time goes in v6:
time: 51.4 us; the launch traced here: 51.2 us
  Pallas kernels  44.7 us (87%)
  local copies, waits for them, and re-layouts  4.49 us (9%)
  between operations  1.95 us (4%)
    pallas_call x1, Pallas kernels, on_device(): pl.pallas_call(functools.partial(kernel, ns, nb), out_shape=(jax.ShapeDty...  44.7 us
    unnamed x10, local copies, waits for them, and re-layouts  4.49 us

profile of v6, /device:TPU:3, one launch (start us, length us, event | category | flops | bytes accessed | tf_op | source)
XLA Modules:
  0.0 51.2 jit_solution(1629678126324372743)
XLA Ops:
  1.9 44.7 %shard_map.156 = (bf16[256,2048]{1,0:T(8,128)(2,1)}, bf16[1,4,2048]{2,1,0:T(4,128)(2,1)}, f32[1,4]{1,0:T(1,128)}, f32[1,2048,128]{2,1,0:T(8,128)}) custom-call(bf16[256,2048]{1,0:T(8,128)(2,1)} %x_in.1, bf16[256,128]{1,0:T(8,128)(2,1)} %keys_in.1, bf16[256,128]{1,0:T(8,128)(2,1)} %queries_in.1, f32[32,256]{1,0:T(8,128)} %bitcast.9, ...), custom_call_target="tpu_custom_call" | custom-call | tf_op jit(solution)/shard_map/pallas_call | solution.py:595
  46.7 0.0 copy-start.1
  46.7 0.0 copy-start
  46.7 2.4 %copy.23 = bf16[256,2048]{1,0:T(8,128)(2,1)} copy(bf16[256,2048]{1,0:T(8,128)(2,1)} %get-tuple-element.16) | data formatting | bytes 2097152
  49.1 0.0 copy-done.1
  49.1 0.0 copy-start.2
  49.1 0.6 %copy.24 = bf16[4,1,2048]{2,0,1:T(4,128)(2,1)} copy(bf16[4,1,2048]{2,0,1:T(4,128)(2,1)S(1)} %bitcast.11) | data formatting | bytes 32768
  49.7 0.0 copy-done.2
  49.7 0.5 copy.25
  50.2 0.0 copy-done
  50.2 1.0 %copy.26 = f32[1,2048,128]{2,1,0:T(8,128)} copy(f32[1,2048,128]{2,1,0:T(8,128)S(1)} %copy-done) | data formatting | bytes 2097152
Async XLA Ops:
  46.7 2.4 %copy-start.1 = (bf16[1,4,2048]{2,1,0:T(4,128)(2,1)S(1)}, bf16[1,4,2048]{2,1,0:T(4,128)(2,1)}, u32[]{:S(2)}) copy-start(bf16[1,4,2048]{2,1,0:T(4,128)(2,1)} %get-tuple-element.9) | copy-start | bytes 49156
  46.7 3.5 %copy-start = (f32[1,2048,128]{2,1,0:T(8,128)S(1)}, f32[1,2048,128]{2,1,0:T(8,128)}, u32[]{:S(2)}) copy-start(f32[1,2048,128]{2,1,0:T(8,128)} %get-tuple-element.19) | copy-start | bytes 3145732
  49.1 0.6 %copy-start.2 = (f32[1,4]{1,0:T(1,128)S(1)}, f32[1,4]{1,0:T(1,128)}, u32[]{:S(2)}) copy-start(f32[1,4]{1,0:T(1,128)} %get-tuple-element.10) | copy-start | bytes 52

commit v7 on v6

--- a/solution.py
+++ b/solution.py
@@ -103,6 +103,10 @@
     v_rs,
     m_ss,
     m_rs,
+    out_made,
+    beam_made,
+    out_sem,
+    beam_sem,
 ):
     g = lax.axis_index("groups")
     s = lax.axis_index("seq")
@@ -227,6 +231,13 @@
             device_id_type=MESH,
         )
 
+    def out_copy(k):
+        return pltpu.make_async_copy(out_made.at[k], out_ref.at[:, lanes_of(k)], out_sem.at[k])
+
+    def beam_copy(kk):
+        rows = pl.ds(pl.multiple_of(kk * LANES, LANES), LANES)
+        return pltpu.make_async_copy(beam_made.at[kk], beam_ref.at[0, rows], beam_sem.at[kk])
+
     def target(k):
         return (b * chunks + k) // dchunks
 
@@ -410,8 +421,8 @@
         keep = pad[:, 0:1]
         dec_add[:, at] = keep * (dec_d[:, at] * read) + dec_add[:, at]
         outer = mm_first(dec_cv[:, at].astype(BF16), dec_k[...].astype(BF16))
-        rows = pl.ds(pl.multiple_of(kk * LANES, LANES), LANES)
-        beam_ref[0, rows, :] = (state * dec_d[steps - 1 : steps, at]).T + outer
+        beam_made[kk] = (state * dec_d[steps - 1 : steps, at]).T + outer
+        beam_copy(kk).start()
 
     def await_and_finish(kk):
         @pl.when(b != owner)
@@ -455,7 +466,8 @@
         @pl.when(s == 0)
         def _():
             up_out[k] = own[k, ROWS : ROWS + n, :]
-            out_ref[:, lanes_of(k)] = inner_ref[k].astype(BF16)
+            out_made[k] = inner_ref[k].astype(BF16)
+            out_copy(k).start()
 
         @pl.when(s > 0)
         def _():
@@ -470,7 +482,8 @@
                     up_sent(k, p).start()
 
             carried = mm(queries_ref[...], up_recv[k].astype(BF16)) * grown[k]
-            out_ref[:, lanes_of(k)] = (inner_ref[k] + carried).astype(BF16)
+            out_made[k] = (inner_ref[k] + carried).astype(BF16)
+            out_copy(k).start()
 
     def share_final(k):
         kk = place(k)
@@ -568,6 +581,18 @@
         return carry
 
     lax.fori_loop(0, chunks, drain, 0)
+
+    def drain_results(k, carry):
+        out_copy(k).wait()
+        return carry
+
+    lax.fori_loop(0, chunks, drain_results, 0)
+
+    def drain_states(kk, carry):
+        beam_copy(kk).wait()
+        return carry
+
+    lax.fori_loop(0, dchunks, drain_states, 0)
 
     @pl.when(relays)
     def _():
@@ -601,7 +626,7 @@
             jax.ShapeDtypeStruct((1, dwidth, n), F32),
         ),
         in_specs=[outside] * 13,
-        out_specs=(spec,) * 4,
+        out_specs=(outside, spec, spec, outside),
         scratch_shapes=[
             *[pltpu.VMEM(a.shape, a.dtype) for a in inputs[:11]],
             *[pltpu.SMEM(a.shape, a.dtype) for a in inputs[11:]],
@@ -636,6 +661,10 @@
             dma((peers,)),
             dma((peers,)),
             dma((peers,)),
+            pltpu.VMEM((chunks, toks, LANES), BF16),
+            pltpu.VMEM((dchunks, LANES, n), F32),
+            dma((chunks,)),
+            dma((dchunks,)),
         ],
         compiler_params=pltpu.CompilerParams(
             collective_id=0, has_side_effects=True, vmem_limit_bytes=60 * 1024 * 1024

time: 51.4 us -> 51.1 us (level)
  no operation moved by 1% of the time
where the time goes in v7:
time: 51.1 us; the launch traced here: 50.9 us
  Pallas kernels  44.5 us (87%)
  local copies, waits for them, and re-layouts  4.49 us (9%)
  between operations  1.95 us (4%)
    pallas_call x1, Pallas kernels, on_device(): pl.pallas_call(functools.partial(kernel, ns, nb), out_shape=(jax.ShapeDty...  44.5 us
    unnamed x10, local copies, waits for them, and re-layouts  4.49 us

profile of v7, /device:TPU:3, one launch (start us, length us, event | category | flops | bytes accessed | tf_op | source)
XLA Modules:
  0.0 50.9 jit_solution(12827702818504561339)
XLA Ops:
  1.9 44.5 %shard_map.156 = (bf16[256,2048]{1,0:T(8,128)(2,1)}, bf16[1,4,2048]{2,1,0:T(4,128)(2,1)}, f32[1,4]{1,0:T(1,128)}, f32[1,2048,128]{2,1,0:T(8,128)}) custom-call(bf16[256,2048]{1,0:T(8,128)(2,1)} %x_in.1, bf16[256,128]{1,0:T(8,128)(2,1)} %keys_in.1, bf16[256,128]{1,0:T(8,128)(2,1)} %queries_in.1, f32[32,256]{1,0:T(8,128)} %bitcast.9, ...), custom_call_target="tpu_custom_call" | custom-call | tf_op jit(solution)/shard_map/pallas_call | solution.py:620
  46.4 0.0 copy-start.1
  46.4 0.0 copy-start
  46.4 2.4 %copy.23 = bf16[256,2048]{1,0:T(8,128)(2,1)} copy(bf16[256,2048]{1,0:T(8,128)(2,1)} %get-tuple-element.16) | data formatting | bytes 2097152
  48.8 0.0 copy-done.1
  48.8 0.0 copy-start.2
  48.8 0.6 %copy.24 = bf16[4,1,2048]{2,0,1:T(4,128)(2,1)} copy(bf16[4,1,2048]{2,0,1:T(4,128)(2,1)S(1)} %bitcast.11) | data formatting | bytes 32768
  49.4 0.0 copy-done.2
  49.4 0.5 %copy.25 = f32[4,1]{0,1:T(1,128)} copy(f32[4,1]{0,1:T(1,128)S(1)} %bitcast.17) | data formatting | bytes 32
  50.0 0.0 copy-done
  50.0 1.0 %copy.26 = f32[1,2048,128]{2,1,0:T(8,128)} copy(f32[1,2048,128]{2,1,0:T(8,128)S(1)} %copy-done) | data formatting | bytes 2097152
Async XLA Ops:
  46.4 2.4 %copy-start.1 = (bf16[1,4,2048]{2,1,0:T(4,128)(2,1)S(1)}, bf16[1,4,2048]{2,1,0:T(4,128)(2,1)}, u32[]{:S(2)}) copy-start(bf16[1,4,2048]{2,1,0:T(4,128)(2,1)} %get-tuple-element.9) | copy-start | bytes 49156
  46.4 3.5 %copy-start = (f32[1,2048,128]{2,1,0:T(8,128)S(1)}, f32[1,2048,128]{2,1,0:T(8,128)}, u32[]{:S(2)}) copy-start(f32[1,2048,128]{2,1,0:T(8,128)} %get-tuple-element.19) | copy-start | bytes 3145732
  48.8 0.6 %copy-start.2 = (f32[1,4]{1,0:T(1,128)S(1)}, f32[1,4]{1,0:T(1,128)}, u32[]{:S(2)}) copy-start(f32[1,4]{1,0:T(1,128)} %get-tuple-element.10) | copy-start | bytes 52
